TPU v7x, 512 devices: a whole 4x8x8 slice. The times are simulated.
512 devices in a mesh: blk: 32 (over x, z), order: 16 (over y, core).
Axes of the slice: x: 4, y: 8, z: 8, core: 2. Of those that a mesh axis runs over, the one named last changes fastest.
Arguments:
- cotangent: bfloat16 [8, 512, 4096], P(None, 'blk', 'order'), may hold values from -6 to 6
- cycle_slot: int32 [512], P('blk'), may hold values from 1 to 4095, as said below
- order_slot: int32 [1024], replicated, may hold values from 0 to 1023, each once
- legendre_healpix: bfloat16 [1024, 512, 1024], P('order', 'blk'), may hold values from -0.25 to 0.25
- legendre_gauss: bfloat16 [1024, 128, 1024], P('order', 'blk'), may hold values from -0.1875 to 0.1875
Outputs:
- gauss_cotangent: float32 [2048, 8, 128], P('order', None, 'blk')
Inputs may be any that keep to these rules, and one draw needn't show every extreme that they name: `cycle_slot`: distinct HEALPix cycle numbers counted from the north pole; both polar end cycles are present. `order_slot`: each wavenumber once.
All inputs are finite; a program needn't handle non-finite values.
Results may differ from a plain program's by a relative error of at most 0.0023.
Values may be sent and summed in bfloat16 or wider, within the bound.
No kernel may reach another device: no remote copies, remote signals or barrier semaphores. Data moves between devices by JAX's collectives and lax.ppermute only.
A program may use at most 64 MiB of HBM per device.

v0:
```python
import math

import jax
import jax.numpy as jnp
from jax import lax
from jax.sharding import PartitionSpec as P

NLON = 2048


def cycle_geometry(cycle_slot, nside, npix):
    nearest = jnp.minimum(jnp.minimum(cycle_slot, nside), 4 * nside - cycle_slot)
    powers = jnp.asarray([2**power_index for power_index in range(nside.bit_length())], jnp.int32)
    rounded = jnp.sum(jnp.where(powers[None, :] < nearest[:, None], powers[None, :], 0), axis=1) + 1
    cycle_length = 4 * rounded
    stride = npix // cycle_length
    shifted = (nearest < nside) | ((cycle_slot - nside) % 2 == 0)
    twice_offset = jnp.where(shifted, stride, 0)
    cycle_scale = 1.0 / jnp.sqrt(cycle_length.astype(jnp.float32))
    return (stride, twice_offset, cycle_scale)


def fourier_sums(data, columns, orders, npix):
    count = orders.shape[0]
    width = math.gcd(count, 128)
    blocks = orders.reshape(count // width, width)

    def one_block(block_orders):
        product = block_orders[:, None] * columns[None, :] % npix
        angle = product.astype(jnp.float32) * (2.0 * math.pi / npix)
        table = jnp.concatenate([jnp.cos(angle), jnp.sin(angle)], axis=0).astype(jnp.bfloat16)
        both = lax.dot_general(
            table, data, (((1,), (1,)), ((), ())), preferred_element_type=jnp.float32
        )
        return (both[:width], both[width:])

    cos_sums, sin_sums = lax.map(one_block, blocks)
    return (cos_sums.reshape(count, -1), sin_sums.reshape(count, -1))


def rotate(cos_sums, sin_sums, orders, twice_offset, cycle_scale, npix):
    product = orders[:, None] * twice_offset[None, :] % (2 * npix)
    phase = product.astype(jnp.float32) * (math.pi / npix)
    cos_phase = jnp.cos(phase)
    sin_phase = jnp.sin(phase)
    real_part = cycle_scale[None, :] * (cos_phase * cos_sums - sin_phase * sin_sums)
    imag_part = -cycle_scale[None, :] * (sin_phase * cos_sums + cos_phase * sin_sums)
    return jnp.stack([real_part, imag_part], axis=1)


def local(cotangent, cycle_slot, order_slot, legendre_healpix, legendre_gauss):
    order_count = lax.axis_size("order")
    order_index = lax.axis_index("order")
    fields, cycle_count, block_pix = cotangent.shape
    npix = block_pix * order_count
    slot_count = legendre_healpix.shape[0]
    degrees = legendre_healpix.shape[2]
    stride, twice_offset, cycle_scale = cycle_geometry(cycle_slot, npix // 4, npix)
    columns = order_index * block_pix + jnp.arange(block_pix, dtype=jnp.int32)
    keep = (columns[None, :] % stride[:, None] == 0).astype(jnp.bfloat16)
    masked = (cotangent * keep[None]).reshape(fields * cycle_count, block_pix)
    row_twice = jnp.tile(twice_offset, fields)
    row_scale = jnp.tile(cycle_scale, fields)
    own_orders = lax.dynamic_slice_in_dim(order_slot, order_index * slot_count, slot_count)
    row_share = fields * cycle_count // order_count
    whole_cycles = lax.all_to_all(masked, "order", split_axis=0, concat_axis=1, tiled=True)
    all_columns = jnp.arange(npix, dtype=jnp.int32)
    cos_sums, sin_sums = fourier_sums(whole_cycles, all_columns, order_slot, npix)
    first_row = order_index * row_share
    share_twice = lax.dynamic_slice_in_dim(row_twice, first_row, row_share)
    share_scale = lax.dynamic_slice_in_dim(row_scale, first_row, row_share)
    coeffs = rotate(cos_sums, sin_sums, order_slot, share_twice, share_scale, npix)
    fourier = lax.all_to_all(coeffs, "order", split_axis=0, concat_axis=2, tiled=True)
    fourier = fourier.reshape(slot_count, 2, fields, cycle_count)
    spectral = jnp.einsum(
        "srl,scfr->slcf",
        legendre_healpix.astype(jnp.float32),
        fourier,
        precision=lax.Precision.HIGHEST,
    )
    degree_index = jnp.arange(degrees, dtype=jnp.int32)
    live = (degree_index[None, :] >= own_orders[:, None]).astype(jnp.float32)
    spectral = spectral * live[:, :, None, None]
    total = lax.psum(spectral, "blk")
    gaussian = jnp.einsum(
        "sgl,slcf->scfg", legendre_gauss.astype(jnp.float32), total, precision=lax.Precision.HIGHEST
    )
    gauss_cycles = gaussian.shape[3]
    flat = gaussian.reshape(slot_count, 2, fields * gauss_cycles)
    longitude = jnp.arange(NLON // order_count * lax.axis_size("order"), dtype=jnp.int32)
    product = longitude[:, None] * own_orders[None, :] % NLON
    angle = product.astype(jnp.float32) * (2.0 * math.pi / NLON)
    values = jnp.dot(jnp.cos(angle), flat[:, 0], precision=lax.Precision.HIGHEST) - jnp.dot(
        jnp.sin(angle), flat[:, 1], precision=lax.Precision.HIGHEST
    )
    return lax.psum_scatter(
        (values * (1.0 / math.sqrt(degrees))).reshape(
            NLON // order_count * lax.axis_size("order"), fields, gauss_cycles
        ),
        "order",
        scatter_dimension=0,
        tiled=True,
    )


def solution(mesh):
    placed = (
        P(None, "blk", "order"),
        P("blk"),
        P(),
        P("order", "blk", None),
        P("order", "blk", None),
    )
    return jax.shard_map(
        local, mesh=mesh, in_specs=placed, out_specs=P("order", None, "blk"), check_vma=False
    )
```

profile of v0, /device:TPU:1, one launch (start us, length us, event | category | flops | bytes accessed | tf_op | source)
XLA Modules:
  0.0 398.3 jit_solution(1925306060677467566)
XLA Ops:
  6.5 0.8 subtract_minimum_fusion
  7.3 0.8 select_reduce_fusion
  8.2 0.8 or_select_fusion
  9.3 1.5 broadcast_multiply_fusion
  10.8 10.2 %all-to-all-start = ((bf16[16,8,256]{2,1,0:T(8,128)(2,1)}), bf16[16,8,256]{2,1,0:T(8,128)(2,1)S(1)}, u32[]{:S(2)}, u32[]{:S(2)}) async-start(bf16[16,8,256]{2,1,0:T(8,128)(2,1)} %bitcast.1), calls=%async_computation | async-start | bytes 131072 | tf_op jit(solution)/shard_map/all_to_all | solution.py:66
  21.1 0.8 dynamic_slice.16
  22.0 6.7 %all-to-all-done = bf16[16,8,256]{2,1,0:T(8,128)(2,1)S(1)} async-done(((bf16[16,8,256]{2,1,0:T(8,128)(2,1)}), bf16[16,8,256]{2,1,0:T(8,128)(2,1)S(1)}, u32[]{:S(2)}, u32[]{:S(2)}) %all-to-all-start) | async-done | bytes 65568 | tf_op jit(solution)/shard_map/all_to_all | solution.py:66
  28.8 82.1 %while.15 = (s32[]{:T(128)}, f32[8,128,8]{1,2,0:T(8,128)S(1)}, f32[8,128,8]{1,2,0:T(8,128)S(1)}, s32[8,128]{1,0:T(8,128)}, bf16[8,4096]{1,0:T(8,128)(2,1)S(1)}, /*index=5*/s32[]{:T(128)}) while((s32[]{:T(128)}, f32[8,128,8]{1,2,0:T(8,128)S(1)}, f32[8,128,8]{1,2,0:T(8,128)S(1)}, s32[8,128]{1,0:T(8,128)}, ...), condition=%wide.region_2.3_spmd.clone, body=%wide.region_1.2_spmd.clone.sunk | while | flops 29360128 | bytes 4286037 | solution.py:37
  29.5 8.9 %cosine_convert_fusion.2 = (bf16[128,4096]{1,0:T(8,128)(2,1)S(1)}, bf16[128,4096]{1,0:T(8,128)(2,1)S(1)}) fusion(s32[128]{0:T(128)S(1)} %fusion.65), kind=kLoop, calls=%fused_computation.15.clone.1 | loop fusion | flops 8388608 | bytes 2097664 | tf_op jit(solution)/shard_map/convert
  39.7 8.9 %cosine_convert_fusion.2 = (bf16[128,4096]{1,0:T(8,128)(2,1)S(1)}, bf16[128,4096]{1,0:T(8,128)(2,1)S(1)}) fusion(s32[128]{0:T(128)S(1)} %fusion.65), kind=kLoop, calls=%fused_computation.15.clone.1 | loop fusion | flops 8388608 | bytes 2097664 | tf_op jit(solution)/shard_map/convert
  49.3 0.7 fusion.65
  50.0 8.9 %cosine_convert_fusion.2 = (bf16[128,4096]{1,0:T(8,128)(2,1)S(1)}, bf16[128,4096]{1,0:T(8,128)(2,1)S(1)}) fusion(s32[128]{0:T(128)S(1)} %fusion.65), kind=kLoop, calls=%fused_computation.15.clone.1 | loop fusion | flops 8388608 | bytes 2097664 | tf_op jit(solution)/shard_map/convert
  59.5 0.7 fusion.65
  60.3 8.9 %cosine_convert_fusion.2 = (bf16[128,4096]{1,0:T(8,128)(2,1)S(1)}, bf16[128,4096]{1,0:T(8,128)(2,1)S(1)}) fusion(s32[128]{0:T(128)S(1)} %fusion.65), kind=kLoop, calls=%fused_computation.15.clone.1 | loop fusion | flops 8388608 | bytes 2097664 | tf_op jit(solution)/shard_map/convert
  70.5 8.9 %cosine_convert_fusion.2 = (bf16[128,4096]{1,0:T(8,128)(2,1)S(1)}, bf16[128,4096]{1,0:T(8,128)(2,1)S(1)}) fusion(s32[128]{0:T(128)S(1)} %fusion.65), kind=kLoop, calls=%fused_computation.15.clone.1 | loop fusion | flops 8388608 | bytes 2097664 | tf_op jit(solution)/shard_map/convert
  80.8 8.9 %cosine_convert_fusion.2 = (bf16[128,4096]{1,0:T(8,128)(2,1)S(1)}, bf16[128,4096]{1,0:T(8,128)(2,1)S(1)}) fusion(s32[128]{0:T(128)S(1)} %fusion.65), kind=kLoop, calls=%fused_computation.15.clone.1 | loop fusion | flops 8388608 | bytes 2097664 | tf_op jit(solution)/shard_map/convert
  91.1 8.9 %cosine_convert_fusion.2 = (bf16[128,4096]{1,0:T(8,128)(2,1)S(1)}, bf16[128,4096]{1,0:T(8,128)(2,1)S(1)}) fusion(s32[128]{0:T(128)S(1)} %fusion.65), kind=kLoop, calls=%fused_computation.15.clone.1 | loop fusion | flops 8388608 | bytes 2097664 | tf_op jit(solution)/shard_map/convert
  101.3 8.9 %cosine_convert_fusion.2 = (bf16[128,4096]{1,0:T(8,128)(2,1)S(1)}, bf16[128,4096]{1,0:T(8,128)(2,1)S(1)}) fusion(s32[128]{0:T(128)S(1)} %fusion.65), kind=kLoop, calls=%fused_computation.15.clone.1 | loop fusion | flops 8388608 | bytes 2097664 | tf_op jit(solution)/shard_map/convert
  110.9 0.9 fusion.36
  112.3 2.2 reshape.359
  114.6 3.4 all-to-all-start.1
  118.2 7.7 %all-to-all-done.1 = f32[16,1,1024]{2,1,0:T(1,128)S(1)} async-done(((f32[16,1,1024]{2,1,0:T(1,128)}), f32[16,1,1024]{2,1,0:T(1,128)S(1)}, u32[]{:S(2)}, u32[]{:S(2)}) %all-to-all-start.1) | async-done | bytes 65568 | tf_op jit(solution)/shard_map/all_to_all | solution.py:73
  126.4 0.8 reduce
  127.2 1.6 reshape.360
  129.5 3.9 multiply_bitcast_fusion
  133.6 171.2 %all-reduce.2.cloned.1.call-done = f32[64,1024,2,8]{1,3,2,0:T(8,128)} async-done(((f32[64,1024,2,8]{1,3,2,0:T(8,128)}), f32[64,1024,2,8]{1,3,2,0:T(8,128)}) %all-reduce.2.cloned.1.call-update) | async-done | bytes 4194320 | tf_op jit(solution)/shard_map/psum | solution.py:84
  304.8 16.1 %fusion.27 = f32[64,2,8,4]{2,3,1,0:T(4,128)S(1)} fusion(f32[64,1024,2,8]{1,3,2,0:T(8,128)} %all-reduce.2.cloned.1.call-done, bf16[64,4,1024]{2,1,0:T(4,128)(2,1)S(1)} %copy-done.1), kind=kOutput, calls=%fused_computation.40 | convolution fusion | flops 50331648 | bytes 4734976 | tf_op jit(solution)/shard_map/sgl,slcf->scfg/dot_general | solution.py:85
  321.0 5.2 %fusion.22 = f32[2048,32]{0,1:T(8,128)S(1)} fusion(s32[64]{0:T(128)S(1)} %dynamic_slice.16, f32[64,2,32]{0,2,1:T(8,128)S(1)} %bitcast.71), kind=kOutput, calls=%fused_computation.35 | convolution fusion | flops 52166656 | bytes 279040 | tf_op jit(solution)/shard_map/dot_general | solution.py:93
  326.2 5.0 %fusion.16 = f32[2048,32]{0,1:T(8,128)S(1)} fusion(f32[2048,32]{0,1:T(8,128)S(1)} %fusion.22, s32[64]{0:T(128)S(1)} %dynamic_slice.16, f32[64,2,32]{0,2,1:T(8,128)S(1)} %bitcast.72), kind=kOutput, calls=%fused_computation.26 | convolution fusion | flops 52297728 | bytes 541184 | tf_op jit(solution)/shard_map/dot_general | solution.py:93
  331.2 1.3 copy.28
  332.5 57.4 %reduce-scatter.4.cloned.1.call-done = f32[128,32]{1,0:T(8,128)} async-done(((f32[2048,32]{1,0:T(8,128)}), f32[128,32]{1,0:T(8,128)}) %reduce-scatter.4.cloned.1.call-update) | async-done | bytes 16400
  390.0 1.5 copy.29
  (50 shorter events, 12.3 us)
Async XLA Ops:
  6.5 123.0 %copy-start = (bf16[64,16,1024]{2,1,0:T(8,128)(2,1)S(1)}, bf16[64,16,1024]{2,1,0:T(8,128)(2,1)}, u32[]{:S(2)}) copy-start(bf16[64,16,1024]{2,1,0:T(8,128)(2,1)} %param.11) | copy-start | bytes 6291460
  10.8 18.0 %all-to-all-start = ((bf16[16,8,256]{2,1,0:T(8,128)(2,1)}), bf16[16,8,256]{2,1,0:T(8,128)(2,1)S(1)}, u32[]{:S(2)}, u32[]{:S(2)}) async-start(bf16[16,8,256]{2,1,0:T(8,128)(2,1)} %bitcast.1), calls=%async_computation | async-start | bytes 131072 | tf_op jit(solution)/shard_map/all_to_all | solution.py:66
  114.6 11.3 %all-to-all-start.1 = ((f32[16,1,1024]{2,1,0:T(1,128)}), f32[16,1,1024]{2,1,0:T(1,128)S(1)}, u32[]{:S(2)}, u32[]{:S(2)}) async-start(f32[16,1,1024]{2,1,0:T(1,128)} %reshape.359), calls=%async_computation.1 | async-start | bytes 131072 | tf_op jit(solution)/shard_map/all_to_all | solution.py:73
  118.0 186.8 %all-reduce.2.cloned.1.call-start = ((), (), s32[]{:S(2)}) async-start(), calls=%async_computation.3 | async-start | bytes 8388608 | tf_op jit(solution)/shard_map/psum | solution.py:84
  133.4 171.5 %copy-start.1 = (bf16[64,4,1024]{2,1,0:T(4,128)(2,1)S(1)}, bf16[64,4,1024]{2,1,0:T(4,128)(2,1)}, u32[]{:S(2)}) copy-start(bf16[64,4,1024]{2,1,0:T(4,128)(2,1)} %param.12) | copy-start | bytes 1572868
  133.4 256.6 %reduce-scatter.4.cloned.1.call-start = ((), (), s32[]{:S(2)}) async-start(), calls=%async_computation.4 | async-start | bytes 1114112
Sparse Core Ops, SparseCore 0:
  133.5 171.2 all-reduce.1
  332.7 57.2 reduce-scatter.3
where the time goes:
time: 400 us; the launch traced here: 398 us
  waiting for transfers between devices  243 us (61%)
  other arithmetic  77.3 us (19%)
  matrix products  35.2 us (9%)
  local copies, waits for them, and re-layouts  15.3 us (4%)
  starting transfers between devices  13.9 us (3%)
  between operations  13.5 us (3%)
    psum x1, waiting for transfers between devices, local(): total = lax.psum(spectral, 'blk')  171 us
    another operation x10, other arithmetic  71.2 us
    unnamed x3, waiting for transfers between devices  57.5 us
    dot_general x1, matrix products, local(): jnp.einsum('sgl,slcf->scfg', legendre_gauss.astype(jnp.float32), total, p...  16.1 us
    all_to_all x1, starting transfers between devices, local(): lax.all_to_all(masked, 'order', split_axis=0, concat_axis=1, tiled=True)  10.2 us
  transfers between devices with their start and end apart: 4, of which 4 were waited for; matrix products, arithmetic and copies ran while one was open for 0% of the time, Pallas kernels for 0%

commit v1 on v0

v1 whole, which is shorter than its diff:
```python
import math

import jax
import jax.numpy as jnp
from jax import lax
from jax.experimental import pallas as pl
from jax.experimental.pallas import tpu as pltpu
from jax.sharding import PartitionSpec as P

NPIX, NLON, NSIDE = 4096, 2048, 1024
FIELDS, ORDERS, DEGREES = 8, 1024, 1024
N_ORDER, N_BLK = 16, 32
SLOTS = ORDERS // N_ORDER
NX, NZA, NZB = 4, 2, 4
NE = NX * NZA
SE = SLOTS // NE
NS = SE // NZB
RB = 16
GB = 4
GROUP_E = [[x * 8 + zb * 2 + za for x in range(NX) for za in range(NZA)] for zb in range(NZB)]
GROUP_Z = [[x * 8 + zb * 2 + za for zb in range(NZB)] for x in range(NX) for za in range(NZA)]
GROUP_ALL = [
    [x * 8 + zb * 2 + za for x in range(NX) for za in range(NZA) for zb in range(NZB)]
]
BF16, F32 = jnp.bfloat16, jnp.float32


def exchange(value, axis, groups=None):
    return lax.all_to_all(
        value, axis, split_axis=0, concat_axis=0, tiled=True, axis_index_groups=groups
    )


def split2(value):
    high = value.astype(BF16)
    return high, (value - high.astype(F32)).astype(BF16)


def params(mib):
    return pltpu.CompilerParams(vmem_limit_bytes=mib << 20)


def cycle_geometry(cycle_slot):
    nearest = jnp.minimum(jnp.minimum(cycle_slot, NSIDE), 4 * NSIDE - cycle_slot)
    powers = jnp.asarray([2**index for index in range(NSIDE.bit_length())], jnp.int32)
    rounded = jnp.sum(jnp.where(powers < nearest, powers, 0)) + 1
    cycle_length = 4 * rounded
    stride = NPIX // cycle_length
    shifted = (nearest < NSIDE) | ((cycle_slot - NSIDE) % 2 == 0)
    twice_offset = jnp.where(shifted, stride, 0)
    cycle_scale = 1.0 / jnp.sqrt(cycle_length.astype(F32))
    return stride, twice_offset, cycle_scale


def table_kernel(ca_ref, sa_ref, cb_ref, sb_ref, out_ref):
    for s in range(SE):
        lanes = slice(s * 128, s * 128 + 128)
        cb, sb = cb_ref[:, lanes], sb_ref[:, lanes]
        for a in range(4):
            ca, sa = ca_ref[0, a : a + 1, lanes], sa_ref[0, a : a + 1, lanes]
            rows = slice(a * 64, a * 64 + 64)
            out_ref[rows, s * 256 : s * 256 + 128] = (ca * cb - sa * sb).astype(BF16)
            out_ref[rows, s * 256 + 128 : s * 256 + 256] = (sa * cb + ca * sb).astype(BF16)


def pixel_table(orders):
    index = jnp.arange(64, dtype=jnp.int32)
    coarse = (index[:, None] * orders[None, :] % 64).astype(F32) * (2.0 * math.pi / 64)
    fine = (index[:, None] * orders[None, :] % NPIX).astype(F32) * (2.0 * math.pi / NPIX)
    ca, sa = jnp.cos(coarse).reshape(16, 4, ORDERS), jnp.sin(coarse).reshape(16, 4, ORDERS)
    part = pl.BlockSpec((1, 4, ORDERS), lambda i: (i, 0, 0))
    whole = pl.BlockSpec((64, ORDERS), lambda i: (0, 0))
    return pl.pallas_call(
        table_kernel,
        grid=(16,),
        out_shape=jax.ShapeDtypeStruct((NPIX, 2 * ORDERS), BF16),
        in_specs=[part, part, whole, whole],
        out_specs=pl.BlockSpec((256, 2 * ORDERS), lambda i: (i, 0)),
        compiler_params=params(32),
    )(ca, sa, jnp.cos(fine), jnp.sin(fine))


def pixel_kernel(stride_ref, x_ref, table_ref, rc_ref, rs_ref, out_ref, acc_ref):
    step = pl.program_id(0)
    column = step * 256 + lax.broadcasted_iota(jnp.int32, (FIELDS, 256), 1)
    keep = (column & (stride_ref[0] - 1)) == 0
    masked = jnp.where(keep, x_ref[0].astype(F32), 0.0).astype(BF16)
    part = jnp.dot(masked, table_ref[...], preferred_element_type=F32)

    @pl.when(step == 0)
    def _():
        acc_ref[...] = part

    @pl.when(step > 0)
    def _():
        acc_ref[...] += part

    @pl.when(step == 15)
    def _():
        rows = []
        for s in range(SE):
            csum = acc_ref[:, s * 256 : s * 256 + 128]
            ssum = acc_ref[:, s * 256 + 128 : s * 256 + 256]
            rc, rs = rc_ref[s : s + 1, :], rs_ref[s : s + 1, :]
            rows.append(rc * csum - rs * ssum)
            rows.append(-(rs * csum + rc * ssum))
        out_ref[...] = jnp.concatenate(rows, axis=0).T


def pixel_sums(stride, x, table, rc, rs):
    return pl.pallas_call(
        pixel_kernel,
        grid=(16,),
        out_shape=jax.ShapeDtypeStruct((128, 128), F32),
        in_specs=[
            pl.BlockSpec(memory_space=pltpu.SMEM),
            pl.BlockSpec((1, FIELDS, 256), lambda i: (i, 0, 0)),
            pl.BlockSpec((256, 2 * ORDERS), lambda i: (i, 0)),
            pl.BlockSpec((SE, 128), lambda i: (0, 0)),
            pl.BlockSpec((SE, 128), lambda i: (0, 0)),
        ],
        out_specs=pl.BlockSpec((128, 128), lambda i: (0, 0)),
        scratch_shapes=[pltpu.VMEM((FIELDS, 2 * ORDERS), F32)],
        compiler_params=params(32),
    )(stride, x, table, rc, rs)


def synthesis_kernel(order_ref, fourier_ref, legendre_ref, out_ref):
    high, low = split2(fourier_ref[...].T)
    degree = lax.broadcasted_iota(jnp.int32, (16, DEGREES), 1)
    for s in range(SE):
        rows = slice(s * 16, s * 16 + 16)
        left = jnp.concatenate([high[rows], low[rows]], axis=0)
        right = jnp.concatenate([legendre_ref[e, s] for e in range(NE)], axis=0)
        both = jnp.dot(left, right, preferred_element_type=F32)
        value = both[:16] + both[16:]
        out_ref[s] = jnp.where(degree >= order_ref[s], value, 0.0).astype(BF16)


def synthesis(orders, fourier, legendre):
    return pl.pallas_call(
        synthesis_kernel,
        out_shape=jax.ShapeDtypeStruct((SE, 16, DEGREES), BF16),
        in_specs=[
            pl.BlockSpec(memory_space=pltpu.SMEM),
            pl.BlockSpec(memory_space=pltpu.VMEM),
            pl.BlockSpec(memory_space=pltpu.VMEM),
        ],
        out_specs=pl.BlockSpec(memory_space=pltpu.VMEM),
        compiler_params=params(32),
    )(orders, fourier, legendre)


def analysis_kernel(spectral_ref, legendre_ref, out_ref):
    total = sum(spectral_ref[z].astype(F32) for z in range(NZB))
    high, low = split2(total.reshape(NS * 16, DEGREES))
    left = jnp.concatenate([high, low], axis=0)
    both = lax.dot_general(
        left, legendre_ref[...], (((1,), (1,)), ((), ())), preferred_element_type=F32
    )
    value = both[: NS * 16] + both[NS * 16 :]
    own = jnp.concatenate([value[:16, :128], value[16:, 128:]], axis=0)
    flipped = own.T
    out_ref[...] = jnp.concatenate(
        [flipped[g * N_BLK : (g + 1) * N_BLK] for g in range(GB)], axis=1
    )


def analysis(spectral, legendre):
    return pl.pallas_call(
        analysis_kernel,
        out_shape=jax.ShapeDtypeStruct((N_BLK, 128), F32),
        compiler_params=params(32),
    )(spectral, legendre)


def longitude_kernel(value_ref, high_ref, low_ref, out_ref):
    high, low = split2(value_ref[...])

    def product(left, right):
        return lax.dot_general(
            left, right, (((0,), (0,)), ((), ())), preferred_element_type=F32
        )

    table = high_ref[...]
    sums = product(high, table) + (product(high, low_ref[...]) + product(low, table))
    for g in range(GB):
        total = None
        for k in range(2 * NS):
            row = g * 32 + k * 8
            piece = sums[row : row + 8, k * 128 : k * 128 + 128]
            total = piece if total is None else total + piece
        out_ref[:, g, :] = total


def longitude_sums(value, high, low):
    return pl.pallas_call(
        longitude_kernel,
        out_shape=jax.ShapeDtypeStruct((FIELDS, GB, 128), F32),
        compiler_params=params(32),
    )(value, high, low)


def longitude_table(order_slot, order_index):
    pair = order_slot.reshape(ORDERS // NS, NS)
    longitude = order_index * 128 + jnp.arange(128, dtype=jnp.int32)
    product = pair[:, :, None] * longitude[None, None, :] % NLON
    angle = product.astype(F32) * (2.0 * math.pi / NLON)
    scale = 1.0 / math.sqrt(DEGREES)
    table = jnp.stack([jnp.cos(angle) * scale, jnp.sin(angle) * -scale], axis=2)
    return split2(table.reshape(ORDERS // NS, NS * 2 * 128))


def local(cotangent, cycle_slot, order_slot, legendre_healpix, legendre_gauss):
    order_index = lax.axis_index("order")
    blk = lax.axis_index("blk")
    e_index = blk // 8 * NZA + blk % NZA

    columns = order_slot.reshape(N_ORDER * NE, SE).T
    table = pixel_table(columns.reshape(ORDERS))
    own_cycle = lax.dynamic_index_in_dim(cycle_slot, order_index, keepdims=False)
    stride, twice_offset, cycle_scale = cycle_geometry(own_cycle)
    phase = (columns * twice_offset % (2 * NPIX)).astype(F32) * (math.pi / NPIX)
    rc, rs = cycle_scale * jnp.cos(phase), cycle_scale * jnp.sin(phase)
    lon_high, lon_low = longitude_table(order_slot, order_index)
    own_orders = lax.dynamic_slice_in_dim(order_slot, order_index * SLOTS + e_index * SE, SE)

    healpix = exchange(legendre_healpix, "blk", GROUP_E).reshape(NE, SE, RB, DEGREES)
    gauss = exchange(legendre_gauss.reshape(N_BLK, NS * GB, DEGREES), "blk", GROUP_ALL)
    gauss = gauss.transpose(1, 0, 2).reshape(NS * GB * N_BLK, DEGREES)

    pixels = exchange(cotangent.transpose(1, 0, 2), "order")
    fourier = pixel_sums(stride.reshape(1), pixels, table, rc, rs)
    fourier = exchange(fourier.reshape(N_ORDER, NE, 128), "order")
    fourier = exchange(fourier.transpose(1, 0, 2), "blk", GROUP_E)
    spectral = synthesis(own_orders, fourier.reshape(NE * RB, 128), healpix)
    spectral = exchange(spectral.reshape(NZB, NS, 16, DEGREES), "blk", GROUP_Z)
    gaussian = analysis(spectral, gauss)
    gaussian = exchange(gaussian, "blk", GROUP_ALL)
    gathered = exchange(jnp.broadcast_to(gaussian, (N_ORDER, N_BLK, 128)), "order")
    result = longitude_sums(gathered.reshape(N_ORDER * N_BLK, 128), lon_high, lon_low)
    return result.transpose(2, 0, 1)


def solution(mesh):
    placed = (
        P(None, "blk", "order"),
        P("blk"),
        P(),
        P("order", "blk", None),
        P("order", "blk", None),
    )
    return jax.shard_map(
        local, mesh=mesh, in_specs=placed, out_specs=P("order", None, "blk"), check_vma=False
    )
```

time: 400 us -> 172 us (0.43)
  waiting for transfers between devices: 243 us -> 61.2 us
  other arithmetic: 77.3 us -> 7.27 us
  matrix products: 35.2 us -> 0 us
  starting transfers between devices: 13.9 us -> 43.5 us
  blocking collectives: 0 us -> 24.2 us
  Pallas kernels: 0 us -> 12.7 us
  between operations: 13.5 us -> 2.98 us
    psum x1 -> x0, waiting for transfers between devices: 171 us -> none  [local(): total = lax.psum(spectral, 'blk')]
    another operation x11 -> x1, other arithmetic: 71.2 us -> 0.07 us  [longitude_table(): table = jnp.stack([jnp.cos(angle) * scale, jnp.sin(angle) * -scale], axis=2)]
    unnamed x3 -> x0, waiting for transfers between devices: 57.5 us -> none
    all_to_all x2 -> x6, waiting for transfers between devices: 14.4 us -> 61.2 us  [exchange(): lax.all_to_all(value, axis, split_axis=0, concat_axis=0, tiled=True, axis...]
    dot_general x12 -> x0, matrix products: 35.2 us -> none  [the longest x1 16.1 us: local(): jnp.einsum('sgl,slcf->scfg', legendre_gauss.astype(jnp.float32), total, p...]
    all_to_all x2 -> x6, starting transfers between devices: 13.6 us -> 43.5 us  [exchange(): lax.all_to_all(value, axis, split_axis=0, concat_axis=0, tiled=True, axis...]
    all_to_all x0 -> x2, blocking collectives: none -> 24.2 us  [exchange(): lax.all_to_all(value, axis, split_axis=0, concat_axis=0, tiled=True, axis...]
    pallas_call x0 -> x5, Pallas kernels: none -> 12.7 us  [the longest x1 4.61 us: pixel_table(): pl.pallas_call(table_kernel, grid=(16,), out_shape=jax.ShapeDtypeStruct((...]
  transfers between devices with their start and end apart: 4 -> 6, of which waited for: 4 -> 5; matrix products, arithmetic and copies ran while one was open for 0% -> 7% of each run, Pallas kernels for 0% -> 4%
where the time goes in v1:
time: 172 us; the launch traced here: 171 us
  waiting for transfers between devices  61.2 us (36%)
  starting transfers between devices  43.5 us (25%)
  blocking collectives  24.2 us (14%)
  local copies, waits for them, and re-layouts  19.1 us (11%)
  Pallas kernels  12.7 us (7%)
  other arithmetic  7.27 us (4%)
  between operations  2.98 us (2%)
    all_to_all x6, waiting for transfers between devices, exchange(): lax.all_to_all(value, axis, split_axis=0, concat_axis=0, tiled=True, axis...  61.2 us
    all_to_all x6, starting transfers between devices, exchange(): lax.all_to_all(value, axis, split_axis=0, concat_axis=0, tiled=True, axis...  43.5 us
    all_to_all x2, blocking collectives, exchange(): lax.all_to_all(value, axis, split_axis=0, concat_axis=0, tiled=True, axis...  24.2 us
    unnamed x9, local copies, waits for them, and re-layouts  13 us
    pallas_call x1, Pallas kernels, pixel_table(): pl.pallas_call(table_kernel, grid=(16,), out_shape=jax.ShapeDtypeStruct((...  4.61 us
    pallas_call x1, Pallas kernels, pixel_sums(): pl.pallas_call(pixel_kernel, grid=(16,), out_shape=jax.ShapeDtypeStruct((...  4.32 us
  transfers between devices with their start and end apart: 6, of which 5 were waited for; matrix products, arithmetic and copies ran while one was open for 7% of the time, Pallas kernels for 4%

profile of v1, /device:TPU:1, one launch (start us, length us, event | category | flops | bytes accessed | tf_op | source)
XLA Modules:
  0.0 170.9 jit_solution(12528380950730991959)
XLA Ops:
  0.0 1.5 copy.32
  1.5 10.2 %all-to-all-start = ((bf16[16,8,256]{2,1,0:T(8,128)(2,1)}), bf16[16,8,256]{2,1,0:T(8,128)(2,1)S(1)}, u32[]{:S(2)}, u32[]{:S(2)}) async-start(bf16[16,8,256]{2,1,0:T(8,128)(2,1)} %bitcast.30), calls=%async_computation | async-start | bytes 131072 | tf_op jit(solution)/shard_map/all_to_all | solution.py:29
  11.7 1.2 dynamic_slice.8
  14.9 1.4 fusion.19
  17.0 0.8 reshape.124
  17.9 1.1 fusion.12
  18.9 2.4 %fusion.14 = (f32[16,4,1024]{2,1,0:T(4,128)S(1)}, f32[16,4,1024]{2,1,0:T(4,128)S(1)}) fusion(s32[1024]{0:T(1024)S(1)} %bitcast.39, s32[16,4]{1,0:T(8,128)S(1)} %multiply_add_fusion), kind=kLoop, calls=%fused_computation.31 | loop fusion | flops 917504 | bytes 528640 | tf_op jit(solution)/shard_map/sin | solution.py:70
  21.4 4.6 %shard_map.64.table_ref = bf16[4096,2048]{1,0:T(8,128)(2,1)S(1)} custom-call(f32[16,4,1024]{2,1,0:T(4,128)S(1)} %get-tuple-element.8.ca_ref, f32[16,4,1024]{2,1,0:T(4,128)S(1)} %get-tuple-element.7.sa_ref, f32[64,1024]{1,0:T(8,128)S(1)} %get-tuple-element.14.cb_ref, f32[64,1024]{1,0:T(8,128)S(1)} %get-tuple-element.13.sb_ref), custom_call_target="tpu_custom_call" | custom-call | tf_op jit(solution)/shard_map/pallas_call | solution.py:73
  26.0 5.7 %copy-done = bf16[4096,2048]{1,0:T(8,128)(2,1)} copy-done((bf16[4096,2048]{1,0:T(8,128)(2,1)}, bf16[4096,2048]{1,0:T(8,128)(2,1)S(1)}, u32[]{:S(2)}) %copy-start) | copy-done | bytes 16777240
  31.8 5.8 %copy-done.1 = bf16[4096,2048]{1,0:T(8,128)(2,1)S(1)} copy-done((bf16[4096,2048]{1,0:T(8,128)(2,1)S(1)}, bf16[4096,2048]{1,0:T(8,128)(2,1)}, u32[]{:S(2)}) %copy-start.1) | copy-done | bytes 16777240
  37.6 4.3 %shard_map.65 = f32[128,128]{1,0:T(8,128)S(1)} custom-call(s32[1]{0:T(128)} %bitcast.1.stride_ref, bf16[16,8,256]{2,1,0:T(8,128)(2,1)S(1)} %all-to-all-done.x_ref, bf16[4096,2048]{1,0:T(8,128)(2,1)S(1)} %copy-done.1, f32[8,128]{1,0:T(8,128)S(1)} %get-tuple-element.12.rc_ref, f32[8,128]{1,0:T(8,128)S(1)} %get-tuple-element.11.rs_ref), custom_call_target="tpu_custom_call" | custom-call | tf_op jit(solution)/shard_map/pallas_call | solution.py:111
  41.9 14.9 %all_to_all.47 = f32[16,8,128]{2,1,0:T(8,128)S(1)} all-to-all(f32[16,8,128]{2,1,0:T(8,128)S(1)} %bitcast.34), channel_id=1, replica_groups=mesh['blk'=32,'order'=16] {'order'}, dimensions={0} | all-to-all | bytes 131072 | tf_op jit(solution)/shard_map/all_to_all | solution.py:29
  56.8 9.3 %all_to_all.48 = f32[8,16,128]{2,1,0:T(8,128)S(1)} all-to-all(f32[8,16,128]{2,1,0:T(8,128)S(1)} %copy.26), channel_id=1, replica_groups={{0,16,128,144,256,272,384,400},{32,48,160,176,288,304,416,432},{64,80,1..., dimensions={0} | all-to-all | bytes 131072 | tf_op jit(solution)/shard_map/all_to_all | solution.py:29
  66.1 3.7 %all-to-all-start.3 = ((bf16[64,16,1024]{2,1,0:T(8,128)(2,1)}), bf16[64,16,1024]{2,1,0:T(8,128)(2,1)S(1)}, u32[]{:S(2)}, u32[]{:S(2)}) async-start(bf16[64,16,1024]{2,1,0:T(8,128)(2,1)} %param.9), calls=%async_computation.3 | async-start | bytes 4194304 | tf_op jit(solution)/shard_map/all_to_all | solution.py:29
  69.9 0.9 reshape.129
  70.8 24.5 %all-to-all-done.3 = bf16[64,16,1024]{2,1,0:T(8,128)(2,1)S(1)} async-done(((bf16[64,16,1024]{2,1,0:T(8,128)(2,1)}), bf16[64,16,1024]{2,1,0:T(8,128)(2,1)S(1)}, u32[]{:S(2)}, u32[]{:S(2)}) %all-to-all-start.3) | async-done | bytes 2097184 | tf_op jit(solution)/shard_map/all_to_all | solution.py:29
  95.3 11.4 %all-to-all-start.5 = ((bf16[32,8,1024]{2,1,0:T(8,128)(2,1)}), bf16[32,8,1024]{2,1,0:T(8,128)(2,1)S(1)}, u32[]{:S(2)}, u32[]{:S(2)}) async-start(bf16[32,8,1024]{2,1,0:T(8,128)(2,1)} %reshape.129), calls=%async_computation.5 | async-start | bytes 1048576 | tf_op jit(solution)/shard_map/all_to_all | solution.py:29
  106.8 1.7 %shard_map.66 = bf16[8,16,1024]{2,1,0:T(8,128)(2,1)} custom-call(s32[8]{0:T(128)S(1)} %dynamic_slice.7.order_ref, f32[128,128]{1,0:T(8,128)S(1)} %bitcast.35, bf16[8,8,16,1024]{3,2,1,0:T(8,128)(2,1)S(1)} %bitcast.31), custom_call_target="tpu_custom_call" | custom-call | tf_op jit(solution)/shard_map/pallas_call | solution.py:141
  108.5 13.0 %all-to-all-done.5 = bf16[32,8,1024]{2,1,0:T(8,128)(2,1)S(1)} async-done(((bf16[32,8,1024]{2,1,0:T(8,128)(2,1)}), bf16[32,8,1024]{2,1,0:T(8,128)(2,1)S(1)}, u32[]{:S(2)}, u32[]{:S(2)}) %all-to-all-start.5) | async-done | bytes 524320 | tf_op jit(solution)/shard_map/all_to_all | solution.py:29
  121.5 4.2 %all-to-all-start.4 = ((bf16[4,2,16,1024]{3,2,1,0:T(8,128)(2,1)}), bf16[4,2,16,1024]{3,2,1,0:T(8,128)(2,1)S(1)}, u32[]{:S(2)}, u32[]{:S(2)}) async-start(bf16[4,2,16,1024]{3,2,1,0:T(8,128)(2,1)} %bitcast.11), calls=%async_computation.4 | async-start | bytes 524288 | tf_op jit(solution)/shard_map/all_to_all | solution.py:29
  125.8 0.3 copy.27
  126.0 7.6 %all-to-all-done.4.spectral_ref = bf16[4,2,16,1024]{3,2,1,0:T(8,128)(2,1)S(1)} async-done(((bf16[4,2,16,1024]{3,2,1,0:T(8,128)(2,1)}), bf16[4,2,16,1024]{3,2,1,0:T(8,128)(2,1)S(1)}, u32[]{:S(2)}, u32[]{:S(2)}) %all-to-all-start.4) | async-done | bytes 262176 | tf_op jit(solution)/shard_map/all_to_all | solution.py:29
  133.7 1.1 shard_map.67
  134.7 7.0 %all-to-all-start.6 = ((f32[32,1,128]{2,1,0:T(1,128)}), f32[32,1,128]{2,1,0:T(1,128)S(1)}, u32[]{:S(2)}, u32[]{:S(2)}) async-start(f32[32,1,128]{2,1,0:T(1,128)} %bitcast.15), calls=%async_computation.6 | async-start | bytes 32768 | tf_op jit(solution)/shard_map/all_to_all | solution.py:29
  142.1 8.2 %all-to-all-done.6 = f32[32,1,128]{2,1,0:T(1,128)S(1)} async-done(((f32[32,1,128]{2,1,0:T(1,128)}), f32[32,1,128]{2,1,0:T(1,128)S(1)}, u32[]{:S(2)}, u32[]{:S(2)}) %all-to-all-start.6) | async-done | bytes 16416 | tf_op jit(solution)/shard_map/all_to_all | solution.py:29
  150.3 0.7 broadcast_in_dim.11
  151.0 7.0 %all-to-all-start.7 = ((f32[16,32,128]{2,1,0:T(8,128)}), f32[16,32,128]{2,1,0:T(8,128)S(1)}, u32[]{:S(2)}, u32[]{:S(2)}) async-start(f32[16,32,128]{2,1,0:T(8,128)} %broadcast_in_dim.11), calls=%async_computation.7 | async-start | bytes 524288 | tf_op jit(solution)/shard_map/all_to_all | solution.py:29
  158.0 2.1 %cosine_multiply_fusion = (f32[512,2,1,128]{3,0,2,1:T(8,128)S(1)}, f32[512,2,1,128]{3,0,2,1:T(8,128)S(1)}) fusion(s32[128]{0:T(128)S(1)} %iota_add_fusion, s32[512,2]{0,1:T(2,128)S(1)} %copy.29), kind=kLoop, calls=%fused_computation.11 | loop fusion | flops 2097152 | bytes 1053184 | tf_op jit(solution)/shard_map/mul | solution.py:210
  160.2 0.8 copy.30
  161.0 0.8 reshape.132
  162.0 7.8 %all-to-all-done.7 = f32[16,32,128]{2,1,0:T(8,128)S(1)} async-done(((f32[16,32,128]{2,1,0:T(8,128)}), f32[16,32,128]{2,1,0:T(8,128)S(1)}, u32[]{:S(2)}, u32[]{:S(2)}) %all-to-all-start.7) | async-done | bytes 262176 | tf_op jit(solution)/shard_map/all_to_all | solution.py:29
  169.9 1.0 shard_map.68
  (17 shorter events, 0.7 us)
Async XLA Ops:
  1.5 30.3 %all-to-all-start = ((bf16[16,8,256]{2,1,0:T(8,128)(2,1)}), bf16[16,8,256]{2,1,0:T(8,128)(2,1)S(1)}, u32[]{:S(2)}, u32[]{:S(2)}) async-start(bf16[16,8,256]{2,1,0:T(8,128)(2,1)} %bitcast.30), calls=%async_computation | async-start | bytes 131072 | tf_op jit(solution)/shard_map/all_to_all | solution.py:29
  26.0 5.7 %copy-start = (bf16[4096,2048]{1,0:T(8,128)(2,1)}, bf16[4096,2048]{1,0:T(8,128)(2,1)S(1)}, u32[]{:S(2)}) copy-start(bf16[4096,2048]{1,0:T(8,128)(2,1)S(1)} %shard_map.64.table_ref) | copy-start | bytes 50331652
  31.8 5.8 %copy-start.1 = (bf16[4096,2048]{1,0:T(8,128)(2,1)S(1)}, bf16[4096,2048]{1,0:T(8,128)(2,1)}, u32[]{:S(2)}) copy-start(bf16[4096,2048]{1,0:T(8,128)(2,1)} %copy-done) | copy-start | bytes 50331652
  66.1 3.7 %copy-start.2 = (bf16[64,4,1024]{2,1,0:T(4,128)(2,1)S(1)}, bf16[64,4,1024]{2,1,0:T(4,128)(2,1)}, u32[]{:S(2)}) copy-start(bf16[64,4,1024]{2,1,0:T(4,128)(2,1)} %param.10) | copy-start | bytes 1572868
  66.1 29.2 %all-to-all-start.3 = ((bf16[64,16,1024]{2,1,0:T(8,128)(2,1)}), bf16[64,16,1024]{2,1,0:T(8,128)(2,1)S(1)}, u32[]{:S(2)}, u32[]{:S(2)}) async-start(bf16[64,16,1024]{2,1,0:T(8,128)(2,1)} %param.9), calls=%async_computation.3 | async-start | bytes 4194304 | tf_op jit(solution)/shard_map/all_to_all | solution.py:29
  69.8 36.8 %copy-start.3 = (s32[1024]{0:T(1024)S(1)}, s32[1024]{0:T(1024)}, u32[]{:S(2)}) copy-start(s32[1024]{0:T(1024)} %param.8) | copy-start | bytes 12292
  95.3 26.2 %all-to-all-start.5 = ((bf16[32,8,1024]{2,1,0:T(8,128)(2,1)}), bf16[32,8,1024]{2,1,0:T(8,128)(2,1)S(1)}, u32[]{:S(2)}, u32[]{:S(2)}) async-start(bf16[32,8,1024]{2,1,0:T(8,128)(2,1)} %reshape.129), calls=%async_computation.5 | async-start | bytes 1048576 | tf_op jit(solution)/shard_map/all_to_all | solution.py:29
  121.5 12.2 %all-to-all-start.4 = ((bf16[4,2,16,1024]{3,2,1,0:T(8,128)(2,1)}), bf16[4,2,16,1024]{3,2,1,0:T(8,128)(2,1)S(1)}, u32[]{:S(2)}, u32[]{:S(2)}) async-start(bf16[4,2,16,1024]{3,2,1,0:T(8,128)(2,1)} %bitcast.11), calls=%async_computation.4 | async-start | bytes 524288 | tf_op jit(solution)/shard_map/all_to_all | solution.py:29
  134.7 15.5 %all-to-all-start.6 = ((f32[32,1,128]{2,1,0:T(1,128)}), f32[32,1,128]{2,1,0:T(1,128)S(1)}, u32[]{:S(2)}, u32[]{:S(2)}) async-start(f32[32,1,128]{2,1,0:T(1,128)} %bitcast.15), calls=%async_computation.6 | async-start | bytes 32768 | tf_op jit(solution)/shard_map/all_to_all | solution.py:29
  151.0 18.8 %all-to-all-start.7 = ((f32[16,32,128]{2,1,0:T(8,128)}), f32[16,32,128]{2,1,0:T(8,128)S(1)}, u32[]{:S(2)}, u32[]{:S(2)}) async-start(f32[16,32,128]{2,1,0:T(8,128)} %broadcast_in_dim.11), calls=%async_computation.7 | async-start | bytes 524288 | tf_op jit(solution)/shard_map/all_to_all | solution.py:29

commit v2 on v0

v2 whole, which is shorter than its diff:
```python
import math

import jax
import jax.numpy as jnp
from jax import lax
from jax.experimental import pallas as pl
from jax.experimental.pallas import tpu as pltpu
from jax.sharding import Mesh, PartitionSpec as P

NPIX, NLON, NSIDE = 4096, 2048, 1024
FIELDS, ORDERS, DEGREES = 8, 1024, 1024
N_ORDER, N_BLK = 16, 32
SLOTS = ORDERS // N_ORDER
NE, NH = 4, 8
SE = SLOTS // NE
NS = SE // NH
RB = 16
GB = 4


BLK = ("xb", "xa", "zb", "za")
E_AXES, H_AXES = ("xa", "za"), ("xb", "zb")


def blk_of(e, h):
    return (h // 4 * 2 + e // 2) * 8 + h % 4 * 2 + e % 2


BF16, F32 = jnp.bfloat16, jnp.float32


def own_e():
    return lax.axis_index(E_AXES)


def exchange(value, axes):
    return lax.all_to_all(value, axes, split_axis=0, concat_axis=0, tiled=True)


def split2(value):
    high = value.astype(BF16)
    return high, (value - high.astype(F32)).astype(BF16)


def params(mib):
    return pltpu.CompilerParams(vmem_limit_bytes=mib << 20)


def pixel_kernel(cycle_ref, x_ref, base_ref, columns_ref, out_ref, acc_ref, fine_ref):
    cycle = cycle_ref[lax.axis_index("order")]
    nearest = jnp.minimum(jnp.minimum(cycle, NSIDE), 4 * NSIDE - cycle)
    rounded, stride = 1, NSIDE
    for index in range(NSIDE.bit_length() - 1):
        above = nearest > 2**index
        rounded = jnp.where(above, 2 ** (index + 1), rounded)
        stride = jnp.where(above, NSIDE // 2 ** (index + 1), stride)

    c0, s0 = base_ref[0, 24:32, :], base_ref[1, 24:32, :]
    for b in range(8):
        c1, s1 = base_ref[0, 16 + b : 17 + b, :], base_ref[1, 16 + b : 17 + b, :]
        fine_ref[0, 8 * b : 8 * b + 8, :] = c1 * c0 - s1 * s0
        fine_ref[1, 8 * b : 8 * b + 8, :] = s1 * c0 + c1 * s0
    acc_ref[...] = jnp.zeros_like(acc_ref)

    def step(block, carry):
        column = block * 256 + lax.broadcasted_iota(jnp.int32, (FIELDS, 256), 1)
        keep = (column & (stride - 1)) == 0
        masked = jnp.where(keep, x_ref[block].astype(F32), 0.0).astype(BF16)
        row1 = pl.ds(block // 2, 1)
        coarse = []
        for a in range(4):
            row0 = pl.ds(8 + block % 2 * 4 + a, 1)
            c1, s1 = base_ref[0, row1, :], base_ref[1, row1, :]
            c0, s0 = base_ref[0, row0, :], base_ref[1, row0, :]
            coarse.append((c1 * c0 - s1 * s0, s1 * c0 + c1 * s0))
        for tile in range(ORDERS // 128):
            lanes = slice(tile * 128, tile * 128 + 128)
            cb, sb = fine_ref[0, :, lanes], fine_ref[1, :, lanes]
            cos_rows = [(ca[:, lanes] * cb - sa[:, lanes] * sb).astype(BF16) for ca, sa in coarse]
            sin_rows = [(sa[:, lanes] * cb + ca[:, lanes] * sb).astype(BF16) for ca, sa in coarse]
            table = jnp.concatenate(
                [jnp.concatenate(cos_rows, axis=0), jnp.concatenate(sin_rows, axis=0)], axis=1
            )
            sums = slice(tile * 256, tile * 256 + 256)
            acc_ref[:, sums] += jnp.dot(masked, table, preferred_element_type=F32)
        return carry

    lax.fori_loop(0, N_ORDER, step, 0)
    shifted = (nearest < NSIDE) | (((cycle - NSIDE) & 1) == 0)
    twice = jnp.where(shifted, stride, 0)
    length = jnp.full((1, ORDERS), 4 * rounded, jnp.int32).astype(F32)
    scale = 1.0 / jnp.sqrt(length)
    phase = ((columns_ref[...] * twice) & (2 * NPIX - 1)).astype(F32) * (math.pi / NPIX)
    rc, rs = scale * jnp.cos(phase), scale * jnp.sin(phase)
    real, imag = [], []
    for tile in range(ORDERS // 128):
        lanes = slice(tile * 128, tile * 128 + 128)
        csum = acc_ref[:, tile * 256 : tile * 256 + 128]
        ssum = acc_ref[:, tile * 256 + 128 : tile * 256 + 256]
        real.append(rc[:, lanes] * csum - rs[:, lanes] * ssum)
        imag.append(-(rs[:, lanes] * csum + rc[:, lanes] * ssum))
    pieces = []
    for tiles in (real, imag):
        flipped = jnp.concatenate(tiles, axis=0).T
        pieces += [flipped[:64], flipped[64:]]
    out_ref[...] = jnp.concatenate(pieces, axis=1)


def pixel_sums(cycle_slot, x, columns):
    unit = jnp.asarray([[512], [64], [8], [1]], jnp.int32) * jnp.arange(8, dtype=jnp.int32)
    angle = (unit.reshape(32, 1) * columns % NPIX).astype(F32) * (2.0 * math.pi / NPIX)
    base = jnp.stack([jnp.cos(angle), jnp.sin(angle)])
    return pl.pallas_call(
        pixel_kernel,
        out_shape=jax.ShapeDtypeStruct((64, 256), F32),
        in_specs=[pl.BlockSpec(memory_space=pltpu.SMEM)]
        + [pl.BlockSpec(memory_space=pltpu.VMEM)] * 3,
        out_specs=pl.BlockSpec(memory_space=pltpu.VMEM),
        scratch_shapes=[
            pltpu.VMEM((FIELDS, 2 * ORDERS), F32),
            pltpu.VMEM((2, 64, ORDERS), F32),
        ],
        compiler_params=params(8),
    )(cycle_slot, x, base, columns)


PART = SE * RB + NH * NS * GB


def parts_kernel(healpix_ref, gauss_ref, *out_refs):
    for k, out_ref in enumerate(out_refs):
        e = own_e() ^ k
        rows = pl.multiple_of(e * (SE * RB), SE * RB)
        out_ref[: SE * RB, :] = healpix_ref[pl.ds(rows, SE * RB), :]
        rows = pl.multiple_of(e * (PART - SE * RB), PART - SE * RB)
        out_ref[SE * RB :, :] = gauss_ref[pl.ds(rows, PART - SE * RB), :]


def exchange_parts(healpix, gauss):
    parts = pl.pallas_call(
        parts_kernel,
        out_shape=[jax.ShapeDtypeStruct((PART, DEGREES), BF16)] * NE,
        in_specs=[pl.BlockSpec(memory_space=pltpu.VMEM)] * 2,
        out_specs=[pl.BlockSpec(memory_space=pltpu.VMEM)] * NE,
        compiler_params=params(10),
    )(healpix.reshape(SLOTS * RB, DEGREES), gauss.reshape(SLOTS * GB, DEGREES))
    result = [parts[0]]
    for k in range(1, NE):
        pairs = [(blk_of(e, h), blk_of(e ^ k, h)) for e in range(NE) for h in range(NH)]
        result.append(lax.ppermute(parts[k], BLK, pairs))
    return result


def synthesis_kernel(order_ref, fourier_ref, *refs):
    part_refs, out_ref = refs[:NE], refs[NE]
    own = own_e()
    parts = [fourier_ref[pl.ds(pl.multiple_of((own ^ k) * RB, RB), RB), :] for k in range(NE)]
    flipped = jnp.concatenate(parts, axis=0).T
    degree = lax.broadcasted_iota(jnp.int32, (16, DEGREES), 1)
    for s in range(SE):
        starts = [c * 128 + s % 2 * 64 + s // 2 * 8 for c in range(2)]
        rows = [flipped[start : start + 8] for start in starts]
        left = jnp.concatenate(split2(jnp.concatenate(rows, axis=0)), axis=0)
        right = jnp.concatenate([ref[s * RB : s * RB + RB, :] for ref in part_refs], axis=0)
        both = jnp.dot(left, right, preferred_element_type=F32)
        value = jnp.where(degree >= order_ref[s], both[:16] + both[16:], 0.0)
        out_ref[s // NS, s % NS * 16 : s % NS * 16 + 16, :] = value.astype(BF16)
    for pair in range(NH // 2):
        start = SE * RB + pair * 16
        both = [ref[start : start + 16, :].astype(F32) for ref in part_refs]
        for side in range(2):
            for k in range(0, NE, 2):
                halves = [rows[side * 8 : side * 8 + 8] for rows in both[k : k + 2]]
                value = jnp.concatenate(halves, axis=0).astype(BF16)
                out_ref[pair * 2 + side, 32 + k * 8 : 48 + k * 8, :] = value


def synthesis(orders, fourier, parts):
    return pl.pallas_call(
        synthesis_kernel,
        out_shape=jax.ShapeDtypeStruct((NH, 64, DEGREES), BF16),
        in_specs=[pl.BlockSpec(memory_space=pltpu.SMEM)]
        + [pl.BlockSpec(memory_space=pltpu.VMEM)] * (1 + NE),
        out_specs=pl.BlockSpec(memory_space=pltpu.VMEM),
        compiler_params=params(10),
    )(orders, fourier, *parts)


def analysis_kernel(sums_ref, out_ref):
    total = sum(sums_ref[h, :32, :].astype(F32) for h in range(NH))
    left = jnp.concatenate(split2(total), axis=0)
    legendre = jnp.concatenate([sums_ref[h, 32:, :] for h in range(NH)], axis=0)
    both = lax.dot_general(
        left, legendre, (((1,), (1,)), ((), ())), preferred_element_type=F32
    )
    both = both[:32] + both[32:]
    high, low = split2(both)
    rest = (both - high.astype(F32) - low.astype(F32)).astype(BF16)
    source = lax.broadcasted_iota(jnp.int32, (256, 256), 0)
    block = (own_e() ^ (source >> 3 & 3)) * NH + (source >> 5)
    wanted = (source & 7) * N_BLK + block
    place = wanted == lax.broadcasted_iota(jnp.int32, (256, 256), 1)
    value = jnp.dot(
        jnp.concatenate([high, low, rest], axis=0),
        jnp.where(place, 1.0, 0.0).astype(BF16),
        preferred_element_type=F32,
    )
    value = value[:32] + value[32:64] + value[64:]
    own = jnp.concatenate([value[:16, :128], value[16:, 128:]], axis=0)
    flipped = own.T
    rows = jnp.concatenate([flipped[g * N_BLK : (g + 1) * N_BLK] for g in range(GB)], axis=1)
    for order in range(N_ORDER):
        out_ref[order] = rows


def analysis(sums):
    return pl.pallas_call(
        analysis_kernel,
        out_shape=jax.ShapeDtypeStruct((N_ORDER, N_BLK, 128), F32),
        compiler_params=params(8),
    )(sums)


def longitude_kernel(value_ref, table_ref, out_ref):
    high, low = split2(value_ref[...])
    table, rest = split2(table_ref[...])

    def product(left, right):
        return lax.dot_general(
            left, right, (((0,), (0,)), ((), ())), preferred_element_type=F32
        )

    sums = product(high, table) + (product(high, rest) + product(low, table))
    for g in range(GB):
        total = None
        for k in range(2 * NS):
            row = g * 32 + k * 8
            piece = sums[row : row + 8, k * 128 : k * 128 + 128]
            total = piece if total is None else total + piece
        out_ref[:, g, :] = total


def longitude_sums(value, table):
    return pl.pallas_call(
        longitude_kernel,
        out_shape=jax.ShapeDtypeStruct((FIELDS, GB, 128), F32),
        compiler_params=params(8),
    )(value, table)


def longitude_table(order_slot, order_index):
    pair = order_slot.reshape(ORDERS // NS, NS)
    longitude = order_index * 128 + jnp.arange(128, dtype=jnp.int32)
    product = pair[:, :, None] * longitude[None, None, :] % NLON
    angle = product.astype(F32) * (2.0 * math.pi / NLON)
    scale = 1.0 / math.sqrt(DEGREES)
    table = jnp.stack([jnp.cos(angle) * scale, jnp.sin(angle) * -scale], axis=2)
    return table.reshape(ORDERS // NS, NS * 2 * 128)


def local(cotangent, cycle_slot, order_slot, legendre_healpix, legendre_gauss):
    order_index = lax.axis_index("order")
    columns = order_slot.reshape(N_ORDER, NE, SE).transpose(2, 1, 0).reshape(1, ORDERS)
    lon_table = longitude_table(order_slot, order_index)
    own_orders = lax.dynamic_slice_in_dim(order_slot, order_index * SLOTS + own_e() * SE, SE)

    pixels = exchange(cotangent.transpose(1, 0, 2), "order")
    parts = exchange_parts(legendre_healpix, legendre_gauss)
    fourier = pixel_sums(cycle_slot, pixels, columns)
    fourier = exchange(fourier, E_AXES + ("order",))
    sums = synthesis(own_orders, fourier, parts)
    sums = exchange(sums, H_AXES)
    gaussian = analysis(sums)
    gathered = exchange(gaussian.reshape(N_ORDER * N_BLK, 128), ("order",) + E_AXES + H_AXES)
    result = longitude_sums(gathered, lon_table)
    return result.transpose(2, 0, 1)


def solution(mesh):
    parts = Mesh(mesh.devices.reshape(2, 2, 4, 2, N_ORDER), BLK + ("order",))
    placed = (
        P(None, BLK, "order"),
        P(BLK),
        P(),
        P("order", BLK, None),
        P("order", BLK, None),
    )
    return jax.shard_map(
        local, mesh=parts, in_specs=placed, out_specs=P("order", None, BLK), check_vma=False
    )
```

time: 400 us -> 126 us (0.32)
  waiting for transfers between devices: 243 us -> 22 us
  other arithmetic: 77.3 us -> 2.92 us
  blocking collectives: 0 us -> 39.7 us
  matrix products: 35.2 us -> 0 us
  starting transfers between devices: 13.9 us -> 41.4 us
  between operations: 13.5 us -> 0.18 us
  Pallas kernels: 0 us -> 11.9 us
  local copies, waits for them, and re-layouts: 15.3 us -> 7.43 us
    psum x1 -> x0, waiting for transfers between devices: 171 us -> none  [local(): total = lax.psum(spectral, 'blk')]
    another operation x11 -> x2, other arithmetic: 71.2 us -> 0.09 us  [the longest x1 0.07 us: longitude_table(): table = jnp.stack([jnp.cos(angle) * scale, jnp.sin(angle) * -scale], axis=2)]
    unnamed x3 -> x0, waiting for transfers between devices: 57.5 us -> none
    all_to_all x0 -> x1, blocking collectives: none -> 39.7 us  [exchange(): return lax.all_to_all(value, axes, split_axis=0, concat_axis=0, tiled=True)]
    dot_general x12 -> x0, matrix products: 35.2 us -> none  [the longest x1 16.1 us: local(): jnp.einsum('sgl,slcf->scfg', legendre_gauss.astype(jnp.float32), total, p...]
    all_to_all x2 -> x3, starting transfers between devices: 13.6 us -> 33.1 us  [exchange(): return lax.all_to_all(value, axes, split_axis=0, concat_axis=0, tiled=True)]
    pallas_call x0 -> x5, Pallas kernels: none -> 11.9 us  [the longest x1 7.06 us: pixel_sums(): pl.pallas_call(pixel_kernel, out_shape=jax.ShapeDtypeStruct((64, 256), F3...]
    ppermute x0 -> x3, starting transfers between devices: none -> 8.36 us  [exchange_parts(): result.append(lax.ppermute(parts[k], BLK, pairs))]
  transfers between devices with their start and end apart: 4 -> 6, of which waited for: 4 -> 2; matrix products, arithmetic and copies ran while one was open for 0% -> 6% of each run, Pallas kernels for 0% -> 7%
where the time goes in v2:
time: 126 us
  starting transfers between devices  41.4 us (33%)
  blocking collectives  39.7 us (32%)
  waiting for transfers between devices  22 us (17%)
  Pallas kernels  11.9 us (9%)
  local copies, waits for them, and re-layouts  7.43 us (6%)
  other arithmetic  2.92 us (2%)
    all_to_all x1, blocking collectives, exchange(): return lax.all_to_all(value, axes, split_axis=0, concat_axis=0, tiled=True)  39.7 us
    all_to_all x3, starting transfers between devices, exchange(): return lax.all_to_all(value, axes, split_axis=0, concat_axis=0, tiled=True)  33.1 us
    all_to_all x3, waiting for transfers between devices, exchange(): return lax.all_to_all(value, axes, split_axis=0, concat_axis=0, tiled=True)  22 us
    ppermute x3, starting transfers between devices, exchange_parts(): result.append(lax.ppermute(parts[k], BLK, pairs))  8.36 us
    pallas_call x1, Pallas kernels, pixel_sums(): pl.pallas_call(pixel_kernel, out_shape=jax.ShapeDtypeStruct((64, 256), F3...  7.06 us
    unnamed x10, local copies, waits for them, and re-layouts  3.11 us
  transfers between devices with their start and end apart: 6, of which 2 were waited for; matrix products, arithmetic and copies ran while one was open for 6% of the time, Pallas kernels for 7%

profile of v2, /device:TPU:1, one launch (start us, length us, event | category | flops | bytes accessed | tf_op | source)
XLA Modules:
  0.0 125.6 jit_solution(17188562099247129618)
XLA Ops:
  0.0 1.5 %copy.29 = bf16[8,16,256]{2,0,1:T(8,128)(2,1)} copy(bf16[8,16,256]{2,1,0:T(8,128)(2,1)} %param.6) | data formatting | bytes 131072 | tf_op args[0]
  1.5 10.2 %all-to-all-start = ((bf16[16,8,256]{2,1,0:T(8,128)(2,1)}), bf16[16,8,256]{2,1,0:T(8,128)(2,1)S(1)}, u32[]{:S(2)}, u32[]{:S(2)}) async-start(bf16[16,8,256]{2,1,0:T(8,128)(2,1)} %bitcast.13), calls=%async_computation | async-start | bytes 131072 | tf_op jit(solution)/shard_map/all_to_all | solution.py:37
  11.7 1.2 reshape.233.gauss_ref
  12.9 1.6 %copy-done = bf16[64,16,1024]{2,1,0:T(8,128)(2,1)S(1)} copy-done((bf16[64,16,1024]{2,1,0:T(8,128)(2,1)S(1)}, bf16[64,16,1024]{2,1,0:T(8,128)(2,1)}, u32[]{:S(2)}) %copy-start) | copy-done | bytes 2097176
  14.4 1.4 %shard_map.65 = (bf16[320,1024]{1,0:T(8,128)(2,1)S(1)}, bf16[320,1024]{1,0:T(8,128)(2,1)}, bf16[320,1024]{1,0:T(8,128)(2,1)}, bf16[320,1024]{1,0:T(8,128)(2,1)}) custom-call(bf16[1024,1024]{1,0:T(8,128)(2,1)S(1)} %bitcast.14, bf16[256,1024]{1,0:T(8,128)(2,1)S(1)} %reshape.233.gauss_ref), custom_call_target="tpu_custom_call" | custom-call | tf_op jit(solution)/shard_map/pallas_call | solution.py:140
  15.8 2.5 %collective-permute-start = (bf16[320,1024]{1,0:T(8,128)(2,1)}, bf16[320,1024]{1,0:T(8,128)(2,1)S(1)}, u32[]{:S(2)}, u32[]{:S(2)}) collective-permute-start(bf16[320,1024]{1,0:T(8,128)(2,1)} %get-tuple-element.10), channel_id=1, source_target_pairs={{0,16},{32,48},{64,80},{96,112},{256,272},{288,304},{320,336},{352... | collective-permute-start | bytes 1966088 | tf_op jit(solution)/shard_map/ppermute | solution.py:150
  18.3 3.1 %collective-permute-start.1 = (bf16[320,1024]{1,0:T(8,128)(2,1)}, bf16[320,1024]{1,0:T(8,128)(2,1)S(1)}, u32[]{:S(2)}, u32[]{:S(2)}) collective-permute-start(bf16[320,1024]{1,0:T(8,128)(2,1)} %get-tuple-element.11), channel_id=1, source_target_pairs={{0,128},{32,160},{64,192},{96,224},{256,384},{288,416},{320,448},{... | collective-permute-start | bytes 1966088 | tf_op jit(solution)/shard_map/ppermute | solution.py:150
  21.4 2.8 %collective-permute-start.2 = (bf16[320,1024]{1,0:T(8,128)(2,1)}, bf16[320,1024]{1,0:T(8,128)(2,1)S(1)}, u32[]{:S(2)}, u32[]{:S(2)}) collective-permute-start(bf16[320,1024]{1,0:T(8,128)(2,1)} %get-tuple-element.12), channel_id=1, source_target_pairs={{0,144},{32,176},{64,208},{96,240},{256,400},{288,432},{320,464},{... | collective-permute-start | bytes 1966088 | tf_op jit(solution)/shard_map/ppermute | solution.py:150
  24.2 0.1 reshape.230
  24.3 0.1 copy.19
  24.4 0.1 mul.155
  24.5 0.1 iota_multiply_fusion
  24.6 0.1 mul.153
  24.7 0.6 fusion.7
  25.3 0.1 reshape.231.columns_ref
  25.4 7.1 %shard_map.64 = f32[64,256]{1,0:T(8,128)S(1)} custom-call(s32[16]{0:T(128)S(1)} %copy-done.1, bf16[16,8,256]{2,1,0:T(8,128)(2,1)S(1)} %all-to-all-done.x_ref, f32[2,32,1024]{2,1,0:T(8,128)S(1)} %pad_maximum_fusion.1.base_ref, s32[1,1024]{1,0:T(1,128)S(1)} %reshape.231.columns_ref), custom_call_target="tpu_custom_call" | custom-call | tf_op jit(solution)/shard_map/pallas_call | solution.py:113
  32.5 0.7 copy.21
  33.2 9.8 %all-to-all-start.1 = ((f32[64,1,256]{2,1,0:T(1,128)}), f32[64,1,256]{2,1,0:T(1,128)S(1)}, u32[]{:S(2)}, u32[]{:S(2)}) async-start(f32[64,1,256]{2,1,0:T(1,128)} %copy.21), calls=%async_computation.1 | async-start | bytes 131072 | tf_op jit(solution)/shard_map/all_to_all | solution.py:37
  43.0 0.1 dynamic_slice.3.order_ref
  43.0 9.0 %all-to-all-done.1 = f32[64,1,256]{2,1,0:T(1,128)S(1)} async-done(((f32[64,1,256]{2,1,0:T(1,128)}), f32[64,1,256]{2,1,0:T(1,128)S(1)}, u32[]{:S(2)}, u32[]{:S(2)}) %all-to-all-start.1) | async-done | bytes 65568 | tf_op jit(solution)/shard_map/all_to_all | solution.py:37
  52.0 1.1 shard_map.66
  53.2 39.7 %all_to_all.32.sums_ref = bf16[8,64,1024]{2,1,0:T(8,128)(2,1)S(1)} all-to-all(bf16[8,64,1024]{2,1,0:T(8,128)(2,1)S(1)} %shard_map.66), channel_id=1, replica_groups=mesh['xb'=2,'xa'=2,'zb'=4,'za'=2,'order'=16] {'xb','zb'}, dimensions={0} | all-to-all | bytes 2097152 | tf_op jit(solution)/shard_map/all_to_all | solution.py:37
  92.9 1.3 %shard_map.67 = f32[16,32,128]{2,1,0:T(8,128)} custom-call(bf16[8,64,1024]{2,1,0:T(8,128)(2,1)S(1)} %all_to_all.32.sums_ref), custom_call_target="tpu_custom_call" | custom-call | tf_op jit(solution)/shard_map/pallas_call | solution.py:217
  94.2 13.1 %all-to-all-start.3 = ((f32[512,1,128]{2,1,0:T(1,128)}), f32[512,1,128]{2,1,0:T(1,128)S(1)}, u32[]{:S(2)}, u32[]{:S(2)}) async-start(f32[512,1,128]{2,1,0:T(1,128)} %bitcast.5), calls=%async_computation.3 | async-start | bytes 524288 | tf_op jit(solution)/shard_map/all_to_all | solution.py:37
  107.3 0.2 mul.160
  107.5 0.1 copy.23
  107.6 2.2 %cosine_multiply_fusion = (f32[512,2,1,128]{3,0,2,1:T(8,128)S(1)}, f32[512,2,1,128]{3,0,2,1:T(8,128)S(1)}) fusion(s32[128]{0:T(128)S(1)} %iota_add_fusion, s32[512,2]{0,1:T(2,128)S(1)} %copy.23), kind=kLoop, calls=%fused_computation.10 | loop fusion | flops 2097152 | bytes 1053184 | tf_op jit(solution)/shard_map/mul | solution.py:257
  109.8 0.1 pad_maximum_fusion
  109.9 0.8 copy.24
  110.7 0.8 reshape.234.table_ref
  111.5 13.0 %all-to-all-done.3 = f32[512,1,128]{2,1,0:T(1,128)S(1)} async-done(((f32[512,1,128]{2,1,0:T(1,128)}), f32[512,1,128]{2,1,0:T(1,128)S(1)}, u32[]{:S(2)}, u32[]{:S(2)}) %all-to-all-start.3) | async-done | bytes 262176 | tf_op jit(solution)/shard_map/all_to_all | solution.py:37
  124.5 1.0 shard_map.68
  (14 shorter events, 0.1 us)
Async XLA Ops:
  0.0 24.5 %copy-start.3 = (s32[4]{0:T(128)S(1)}, s32[4]{0:T(128)}, u32[]{:S(2)}) copy-start(s32[4]{0:T(128)} %constant.68) | copy-start | bytes 52
  0.0 24.2 %copy-start.2 = (s32[1024]{0:T(1024)S(1)}, s32[1024]{0:T(1024)}, u32[]{:S(2)}) copy-start(s32[1024]{0:T(1024)} %param.8) | copy-start | bytes 12292
  1.5 23.9 %all-to-all-start = ((bf16[16,8,256]{2,1,0:T(8,128)(2,1)}), bf16[16,8,256]{2,1,0:T(8,128)(2,1)S(1)}, u32[]{:S(2)}, u32[]{:S(2)}) async-start(bf16[16,8,256]{2,1,0:T(8,128)(2,1)} %bitcast.13), calls=%async_computation | async-start | bytes 131072 | tf_op jit(solution)/shard_map/all_to_all | solution.py:37
  11.7 13.7 %copy-start.1 = (s32[16]{0:T(128)S(1)}, s32[16]{0:T(128)}, u32[]{:S(2)}) copy-start(s32[16]{0:T(128)} %cycle_ref.1) | copy-start | bytes 196
  12.9 1.6 %copy-start = (bf16[64,16,1024]{2,1,0:T(8,128)(2,1)S(1)}, bf16[64,16,1024]{2,1,0:T(8,128)(2,1)}, u32[]{:S(2)}) copy-start(bf16[64,16,1024]{2,1,0:T(8,128)(2,1)} %param.9) | copy-start | bytes 6291460
  15.8 36.2 %collective-permute-start = (bf16[320,1024]{1,0:T(8,128)(2,1)}, bf16[320,1024]{1,0:T(8,128)(2,1)S(1)}, u32[]{:S(2)}, u32[]{:S(2)}) collective-permute-start(bf16[320,1024]{1,0:T(8,128)(2,1)} %get-tuple-element.10), channel_id=1, source_target_pairs={{0,16},{32,48},{64,80},{96,112},{256,272},{288,304},{320,336},{352... | collective-permute-start | bytes 1966088 | tf_op jit(solution)/shard_map/ppermute | solution.py:150
  18.3 33.7 %collective-permute-start.1 = (bf16[320,1024]{1,0:T(8,128)(2,1)}, bf16[320,1024]{1,0:T(8,128)(2,1)S(1)}, u32[]{:S(2)}, u32[]{:S(2)}) collective-permute-start(bf16[320,1024]{1,0:T(8,128)(2,1)} %get-tuple-element.11), channel_id=1, source_target_pairs={{0,128},{32,160},{64,192},{96,224},{256,384},{288,416},{320,448},{... | collective-permute-start | bytes 1966088 | tf_op jit(solution)/shard_map/ppermute | solution.py:150
  21.4 30.6 %collective-permute-start.2 = (bf16[320,1024]{1,0:T(8,128)(2,1)}, bf16[320,1024]{1,0:T(8,128)(2,1)S(1)}, u32[]{:S(2)}, u32[]{:S(2)}) collective-permute-start(bf16[320,1024]{1,0:T(8,128)(2,1)} %get-tuple-element.12), channel_id=1, source_target_pairs={{0,144},{32,176},{64,208},{96,240},{256,400},{288,432},{320,464},{... | collective-permute-start | bytes 1966088 | tf_op jit(solution)/shard_map/ppermute | solution.py:150
  33.2 18.9 %all-to-all-start.1 = ((f32[64,1,256]{2,1,0:T(1,128)}), f32[64,1,256]{2,1,0:T(1,128)S(1)}, u32[]{:S(2)}, u32[]{:S(2)}) async-start(f32[64,1,256]{2,1,0:T(1,128)} %copy.21), calls=%async_computation.1 | async-start | bytes 131072 | tf_op jit(solution)/shard_map/all_to_all | solution.py:37
  94.2 30.3 %all-to-all-start.3 = ((f32[512,1,128]{2,1,0:T(1,128)}), f32[512,1,128]{2,1,0:T(1,128)S(1)}, u32[]{:S(2)}, u32[]{:S(2)}) async-start(f32[512,1,128]{2,1,0:T(1,128)} %bitcast.5), calls=%async_computation.3 | async-start | bytes 524288 | tf_op jit(solution)/shard_map/all_to_all | solution.py:37

commit v3 on v2

v3 whole, which is shorter than its diff:
```python
import math

import jax
import jax.numpy as jnp
from jax import lax
from jax.experimental import pallas as pl
from jax.experimental.pallas import tpu as pltpu
from jax.sharding import Mesh, PartitionSpec as P

NPIX, NLON, NSIDE = 4096, 2048, 1024
FIELDS, ORDERS, DEGREES = 8, 1024, 1024
N_ORDER, N_BLK = 16, 32
SLOTS = ORDERS // N_ORDER
NX, NZ = 4, 8
SE = SLOTS // NX
NS = SE // NZ
RB = 16
GB = 4
BLK = ("x", "z")


BF16, F32 = jnp.bfloat16, jnp.float32


def exchange(value, axes):
    return lax.all_to_all(value, axes, split_axis=0, concat_axis=0, tiled=True)


def split2(value):
    high = value.astype(BF16)
    return high, (value - high.astype(F32)).astype(BF16)


def params(mib):
    return pltpu.CompilerParams(vmem_limit_bytes=mib << 20)


def pixel_kernel(cycle_ref, x_ref, base_ref, columns_ref, out_ref, acc_ref, fine_ref, fold_ref):
    cycle = cycle_ref[lax.axis_index("order")]
    nearest = jnp.minimum(jnp.minimum(cycle, NSIDE), 4 * NSIDE - cycle)
    rounded, stride = 1, NSIDE
    for index in range(NSIDE.bit_length() - 1):
        above = nearest > 2**index
        rounded = jnp.where(above, 2 ** (index + 1), rounded)
        stride = jnp.where(above, NSIDE // 2 ** (index + 1), stride)

    lane = lax.broadcasted_iota(jnp.int32, (FIELDS, 256), 1)
    pixels = []
    for block in range(N_ORDER):
        keep = ((block * 256 + lane) & (stride - 1)) == 0
        pixels.append(jnp.where(keep, x_ref[block].astype(F32), 0.0))
    backward = [15, 14, 13, 12, 7, 6, 5, 4]
    row = lax.broadcasted_iota(jnp.int32, (256, 256), 0)
    col = lax.broadcasted_iota(jnp.int32, (256, 256), 1)
    turn = jnp.where(row + col == 256, 1.0, 0.0).astype(BF16)
    turned = jnp.dot(
        jnp.concatenate([pixels[block] for block in backward], axis=0).astype(BF16),
        turn,
        preferred_element_type=F32,
    )
    for block in range(4):
        first, second = turned[block * 8 : block * 8 + 8], turned[block * 8 + 32 : block * 8 + 40]
        if block:
            first = jnp.where(lane == 0, pixels[16 - block][:, :1], first)
            second = jnp.where(lane == 0, pixels[8 - block][:, :1], second)
        near, far = pixels[block], pixels[8 + block]
        even, odd = near + first, near - first
        other_even, other_odd = second + far, second - far
        cos_rows = split2(even + other_even) + split2(even - other_even)
        sin_rows = split2(odd - other_odd) + split2(odd + other_odd)
        fold_ref[block, 0] = jnp.concatenate(cos_rows, axis=0)
        fold_ref[block, 1] = jnp.concatenate(sin_rows, axis=0)

    c0, s0 = base_ref[0, 18:26, :], base_ref[1, 18:26, :]
    for b in range(8):
        c1, s1 = base_ref[0, 10 + b : 11 + b, :], base_ref[1, 10 + b : 11 + b, :]
        fine_ref[0, 8 * b : 8 * b + 8, :] = c1 * c0 - s1 * s0
        fine_ref[1, 8 * b : 8 * b + 8, :] = s1 * c0 + c1 * s0
    acc_ref[...] = jnp.zeros_like(acc_ref)

    def step(block, carry):
        row1 = pl.ds(block // 2, 1)
        coarse = []
        for a in range(4):
            row0 = pl.ds(2 + block % 2 * 4 + a, 1)
            c1, s1 = base_ref[0, row1, :], base_ref[1, row1, :]
            c0, s0 = base_ref[0, row0, :], base_ref[1, row0, :]
            coarse.append((c1 * c0 - s1 * s0, s1 * c0 + c1 * s0))
        cos_left, sin_left = fold_ref[block, 0], fold_ref[block, 1]
        for tile in range(ORDERS // 256):
            lanes = slice(tile * 256, tile * 256 + 256)
            cb, sb = fine_ref[0, :, lanes], fine_ref[1, :, lanes]
            cos_rows = [(ca[:, lanes] * cb - sa[:, lanes] * sb).astype(BF16) for ca, sa in coarse]
            table = jnp.concatenate(cos_rows, axis=0)
            acc_ref[0, :, lanes] += jnp.dot(cos_left, table, preferred_element_type=F32)
            sin_rows = [(sa[:, lanes] * cb + ca[:, lanes] * sb).astype(BF16) for ca, sa in coarse]
            table = jnp.concatenate(sin_rows, axis=0)
            acc_ref[1, :, lanes] += jnp.dot(sin_left, table, preferred_element_type=F32)
        return carry

    lax.fori_loop(0, 4, step, 0)
    columns = columns_ref[...]
    is_odd = (columns & 1) == 1
    quarter = columns & 3
    cos_quarter = jnp.where(quarter == 0, 1.0, jnp.where(quarter == 2, -1.0, 0.0))
    sin_quarter = jnp.where(quarter == 1, 1.0, jnp.where(quarter == 3, -1.0, 0.0))
    one, three = pixels[4][:, :1], pixels[12][:, :1]
    sums = []
    for part, extra in ((0, (one + three) * cos_quarter), (1, (one - three) * sin_quarter)):
        even = acc_ref[part, 0:8, :] + acc_ref[part, 8:16, :]
        odd = acc_ref[part, 16:24, :] + acc_ref[part, 24:32, :]
        sums.append(jnp.where(is_odd, odd, even) + extra)
    csum, ssum = sums
    shifted = (nearest < NSIDE) | (((cycle - NSIDE) & 1) == 0)
    twice = jnp.where(shifted, stride, 0)
    length = jnp.full((1, ORDERS), 4 * rounded, jnp.int32).astype(F32)
    scale = 1.0 / jnp.sqrt(length)
    phase = ((columns * twice) & (2 * NPIX - 1)).astype(F32) * (math.pi / NPIX)
    rc, rs = scale * jnp.cos(phase), scale * jnp.sin(phase)
    pieces = []
    for value in (rc * csum - rs * ssum, -(rs * csum + rc * ssum)):
        tiles = [value[:, tile * 128 : tile * 128 + 128] for tile in range(8)]
        flipped = jnp.concatenate(tiles, axis=0).T
        pieces += [flipped[:64], flipped[64:]]
    out_ref[...] = jnp.concatenate(pieces, axis=1)


def pixel_sums(cycle_slot, x, columns):
    steps = [512 * a for a in range(2)] + [64 * a for a in range(8)]
    steps = jnp.asarray(steps + [8 * b for b in range(8)] + list(range(8)), jnp.int32)
    angle = (steps[:, None] * columns % NPIX).astype(F32) * (2.0 * math.pi / NPIX)
    base = jnp.stack([jnp.cos(angle), jnp.sin(angle)])
    return pl.pallas_call(
        pixel_kernel,
        out_shape=jax.ShapeDtypeStruct((64, 256), F32),
        in_specs=[pl.BlockSpec(memory_space=pltpu.SMEM)]
        + [pl.BlockSpec(memory_space=pltpu.VMEM)] * 3,
        out_specs=pl.BlockSpec(memory_space=pltpu.VMEM),
        scratch_shapes=[
            pltpu.VMEM((2, 4 * FIELDS, ORDERS), F32),
            pltpu.VMEM((2, 64, ORDERS), F32),
            pltpu.VMEM((4, 2, 4 * FIELDS, 256), BF16),
        ],
        compiler_params=params(8),
    )(cycle_slot, x, base, columns)


def parts_kernel(healpix_ref, *refs):
    out_refs, sems = refs[:NX], refs[NX]
    copies = []
    for k in (1, 2, 3, 0):
        rows = pl.multiple_of((lax.axis_index("x") ^ k) * (SE * RB), SE * RB)
        source = healpix_ref.at[pl.ds(rows, SE * RB), :]
        copies.append(pltpu.make_async_copy(source, out_refs[k], sems.at[k]))
    for copy in copies:
        copy.start()
    for copy in copies:
        copy.wait()


def exchange_parts(healpix):
    parts = pl.pallas_call(
        parts_kernel,
        out_shape=[jax.ShapeDtypeStruct((SE * RB, DEGREES), BF16)] * NX,
        in_specs=[pl.BlockSpec(memory_space=pl.ANY)],
        out_specs=[pl.BlockSpec(memory_space=pltpu.VMEM)] * NX,
        scratch_shapes=[pltpu.SemaphoreType.DMA((NX,))],
        compiler_params=params(10),
    )(healpix.reshape(SLOTS * RB, DEGREES))
    result = [parts[0]]
    for k in range(1, NX):
        result.append(lax.ppermute(parts[k], "x", [(x, x ^ k) for x in range(NX)]))
    return result


def synthesis_kernel(order_ref, fourier_ref, *refs):
    part_refs, out_ref = refs[:NX], refs[NX]
    own = lax.axis_index("x")
    parts = [fourier_ref[pl.ds(pl.multiple_of((own ^ k) * RB, RB), RB), :] for k in range(NX)]
    flipped = jnp.concatenate(parts, axis=0).T
    degree = lax.broadcasted_iota(jnp.int32, (16, DEGREES), 1)
    for s in range(SE):
        starts = [c * 128 + s % 2 * 64 + s // 2 * 8 for c in range(2)]
        rows = [flipped[start : start + 8] for start in starts]
        left = jnp.concatenate(split2(jnp.concatenate(rows, axis=0)), axis=0)
        right = jnp.concatenate([ref[s * RB : s * RB + RB, :] for ref in part_refs], axis=0)
        both = jnp.dot(left, right, preferred_element_type=F32)
        value = jnp.where(degree >= order_ref[s], both[:16] + both[16:], 0.0)
        out_ref[s // NS, s % NS * 16 : s % NS * 16 + 16, :] = value.astype(BF16)


def synthesis(orders, fourier, parts):
    return pl.pallas_call(
        synthesis_kernel,
        out_shape=jax.ShapeDtypeStruct((NZ, NS * 16, DEGREES), BF16),
        in_specs=[pl.BlockSpec(memory_space=pltpu.SMEM)]
        + [pl.BlockSpec(memory_space=pltpu.VMEM)] * (1 + NX),
        out_specs=pl.BlockSpec(memory_space=pltpu.VMEM),
        compiler_params=params(10),
    )(orders, fourier, *parts)


def analysis_kernel(sums_ref, legendre_ref, out_ref):
    total = sum(sums_ref[h].astype(F32) for h in range(NZ))
    left = jnp.concatenate(split2(total), axis=0)
    both = lax.dot_general(
        left, legendre_ref[...], (((1,), (1,)), ((), ())), preferred_element_type=F32
    )
    both = both[:32] + both[32:]
    high, low = split2(both)
    rest = (both - high.astype(F32) - low.astype(F32)).astype(BF16)
    source = lax.broadcasted_iota(jnp.int32, (256, 256), 0)
    wanted = (source & 7) * N_BLK + (source >> 3)
    place = wanted == lax.broadcasted_iota(jnp.int32, (256, 256), 1)
    value = jnp.dot(
        jnp.concatenate([high, low, rest], axis=0),
        jnp.where(place, 1.0, 0.0).astype(BF16),
        preferred_element_type=F32,
    )
    value = value[:32] + value[32:64] + value[64:]
    own = jnp.concatenate([value[:16, :128], value[16:, 128:]], axis=0)
    flipped = own.T
    rows = jnp.concatenate([flipped[g * N_BLK : (g + 1) * N_BLK] for g in range(GB)], axis=1)
    for blk in range(N_BLK):
        out_ref[blk] = jnp.broadcast_to(rows[blk : blk + 1], (N_ORDER, 128))


def analysis(sums, legendre):
    return pl.pallas_call(
        analysis_kernel,
        out_shape=jax.ShapeDtypeStruct((N_BLK, N_ORDER, 128), F32),
        compiler_params=params(8),
    )(sums, legendre)


def longitude_kernel(value_ref, table_ref, out_ref):
    high, low = split2(value_ref[...])
    table, rest = split2(table_ref[...])

    def product(left, right):
        return lax.dot_general(
            left, right, (((0,), (0,)), ((), ())), preferred_element_type=F32
        )

    sums = product(high, table) + (product(high, rest) + product(low, table))
    for g in range(GB):
        total = None
        for k in range(2 * NS):
            row = g * 32 + k * 8
            piece = sums[row : row + 8, k * 128 : k * 128 + 128]
            total = piece if total is None else total + piece
        out_ref[:, g, :] = total


def longitude_sums(value, table):
    return pl.pallas_call(
        longitude_kernel,
        out_shape=jax.ShapeDtypeStruct((FIELDS, GB, 128), F32),
        compiler_params=params(8),
    )(value, table)


def longitude_table(order_slot, order_index):
    pair = order_slot.reshape(N_ORDER, N_BLK, NS).transpose(1, 0, 2)
    pair = pair.reshape(ORDERS // NS, NS)
    longitude = order_index * 128 + jnp.arange(128, dtype=jnp.int32)
    product = pair[:, :, None] * longitude[None, None, :] % NLON
    angle = product.astype(F32) * (2.0 * math.pi / NLON)
    scale = 1.0 / math.sqrt(DEGREES)
    table = jnp.stack([jnp.cos(angle) * scale, jnp.sin(angle) * -scale], axis=2)
    return table.reshape(ORDERS // NS, NS * 2 * 128)


def local(cotangent, cycle_slot, order_slot, legendre_healpix, legendre_gauss):
    order_index = lax.axis_index("order")
    columns = order_slot.reshape(N_ORDER, NX, SE).transpose(2, 1, 0).reshape(1, ORDERS)
    lon_table = longitude_table(order_slot, order_index)
    first_slot = order_index * SLOTS + lax.axis_index("x") * SE
    own_orders = lax.dynamic_slice_in_dim(order_slot, first_slot, SE)

    parts = exchange_parts(legendre_healpix)
    gauss = exchange(legendre_gauss.reshape(N_BLK, NS * GB, DEGREES), BLK)
    gauss, cotangent = lax.optimization_barrier((gauss, cotangent))
    pixels = exchange(cotangent.transpose(1, 0, 2), "order")
    fourier = pixel_sums(cycle_slot, pixels, columns)
    fourier = exchange(fourier, ("x", "order"))
    sums = synthesis(own_orders, fourier, parts)
    sums = exchange(sums, "z")
    gaussian = analysis(sums, gauss.reshape(N_BLK * NS * GB, DEGREES))
    gathered = exchange(gaussian.reshape(N_BLK * N_ORDER, 128), BLK + ("order",))
    result = longitude_sums(gathered, lon_table)
    return result.transpose(2, 0, 1)


def solution(mesh):
    parts = Mesh(mesh.devices.reshape(NX, NZ, N_ORDER), BLK + ("order",))
    placed = (
        P(None, BLK, "order"),
        P(BLK),
        P(),
        P("order", BLK, None),
        P("order", BLK, None),
    )
    return jax.shard_map(
        local, mesh=parts, in_specs=placed, out_specs=P("order", None, BLK), check_vma=False
    )
```

time: 126 us -> 119 us (0.944)
  blocking collectives: 39.7 us -> 20.5 us
  waiting for transfers between devices: 22 us -> 32.3 us
  starting transfers between devices: 41.4 us -> 48.4 us
  Pallas kernels: 11.9 us -> 7.69 us
  local copies, waits for them, and re-layouts: 7.43 us -> 6.15 us
    all_to_all x1, blocking collectives: 39.7 us -> 20.5 us  [exchange(): return lax.all_to_all(value, axes, split_axis=0, concat_axis=0, tiled=True)]
    all_to_all x3 -> x4, waiting for transfers between devices: 22 us -> 32.3 us  [exchange(): return lax.all_to_all(value, axes, split_axis=0, concat_axis=0, tiled=True)]
    all_to_all x3 -> x4, starting transfers between devices: 33.1 us -> 38.8 us  [exchange(): return lax.all_to_all(value, axes, split_axis=0, concat_axis=0, tiled=True)]
    pallas_call x1, Pallas kernels: 7.06 us -> 2.84 us  [pixel_sums(): pl.pallas_call(pixel_kernel, out_shape=jax.ShapeDtypeStruct((64, 256), F3...]
    unnamed x10 -> x11, local copies, waits for them, and re-layouts: 3.11 us -> 0.02 us
  transfers between devices with their start and end apart: 6 -> 7, of which waited for: 2 -> 4; matrix products, arithmetic and copies ran while one was open for 6% -> 6% of each run, Pallas kernels for 7% -> 4%
where the time goes in v3:
time: 119 us; the launch traced here: 118 us
  starting transfers between devices  48.4 us (41%)
  waiting for transfers between devices  32.3 us (27%)
  blocking collectives  20.5 us (17%)
  Pallas kernels  7.69 us (6%)
  local copies, waits for them, and re-layouts  6.15 us (5%)
  other arithmetic  2.83 us (2%)
    all_to_all x4, starting transfers between devices, exchange(): return lax.all_to_all(value, axes, split_axis=0, concat_axis=0, tiled=True)  38.8 us
    all_to_all x4, waiting for transfers between devices, exchange(): return lax.all_to_all(value, axes, split_axis=0, concat_axis=0, tiled=True)  32.3 us
    all_to_all x1, blocking collectives, exchange(): return lax.all_to_all(value, axes, split_axis=0, concat_axis=0, tiled=True)  20.5 us
    ppermute x3, starting transfers between devices, exchange_parts(): result.append(lax.ppermute(parts[k], 'x', [(x, x ^ k) for x in range(NX)]))  9.58 us
    pallas_call x1, Pallas kernels, pixel_sums(): pl.pallas_call(pixel_kernel, out_shape=jax.ShapeDtypeStruct((64, 256), F3...  2.84 us
  transfers between devices with their start and end apart: 7, of which 4 were waited for; matrix products, arithmetic and copies ran while one was open for 6% of the time, Pallas kernels for 4%

profile of v3, /device:TPU:1, one launch (start us, length us, event | category | flops | bytes accessed | tf_op | source)
XLA Modules:
  0.0 118.1 jit_solution(14505514740130010317)
XLA Ops:
  0.0 2.1 %reshape.217 = bf16[32,8,1024]{2,1,0:T(8,128)(2,1)} reshape(bf16[64,4,1024]{2,1,0:T(4,128)(2,1)} %param.10) | data formatting | bytes 1048576 | tf_op jit(solution)/shard_map/reshape | solution.py:282
  2.2 13.8 %all-to-all-start = ((bf16[32,8,1024]{2,1,0:T(8,128)(2,1)}), bf16[32,8,1024]{2,1,0:T(8,128)(2,1)S(1)}, u32[]{:S(2)}, u32[]{:S(2)}) async-start(bf16[32,8,1024]{2,1,0:T(8,128)(2,1)} %reshape.217), calls=%async_computation | async-start | bytes 1048576 | tf_op jit(solution)/shard_map/all_to_all | solution.py:26
  16.0 1.4 %shard_map.65 = (bf16[256,1024]{1,0:T(8,128)(2,1)S(1)}, bf16[256,1024]{1,0:T(8,128)(2,1)}, bf16[256,1024]{1,0:T(8,128)(2,1)}, bf16[256,1024]{1,0:T(8,128)(2,1)}) custom-call(bf16[1024,1024]{1,0:T(8,128)(2,1)S(1)} %bitcast.18), custom_call_target="tpu_custom_call" | custom-call | tf_op jit(solution)/shard_map/pallas_call | solution.py:162
  17.4 3.1 %collective-permute-start = (bf16[256,1024]{1,0:T(8,128)(2,1)}, bf16[256,1024]{1,0:T(8,128)(2,1)S(1)}, u32[]{:S(2)}, u32[]{:S(2)}) collective-permute-start(bf16[256,1024]{1,0:T(8,128)(2,1)} %get-tuple-element.13), channel_id=1, source_target_pairs={{0,128},{128,0},{256,384},{384,256},{1,129},{129,1},{257,385},{385... | collective-permute-start | bytes 1572872 | tf_op jit(solution)/shard_map/ppermute | solution.py:172
  20.6 4.3 %collective-permute-start.1 = (bf16[256,1024]{1,0:T(8,128)(2,1)}, bf16[256,1024]{1,0:T(8,128)(2,1)S(1)}, u32[]{:S(2)}, u32[]{:S(2)}) collective-permute-start(bf16[256,1024]{1,0:T(8,128)(2,1)} %get-tuple-element.14), channel_id=1, source_target_pairs={{0,256},{128,384},{256,0},{384,128},{1,257},{129,385},{257,1},{385... | collective-permute-start | bytes 1572872 | tf_op jit(solution)/shard_map/ppermute | solution.py:172
  24.9 2.1 %collective-permute-start.2 = (bf16[256,1024]{1,0:T(8,128)(2,1)}, bf16[256,1024]{1,0:T(8,128)(2,1)S(1)}, u32[]{:S(2)}, u32[]{:S(2)}) collective-permute-start(bf16[256,1024]{1,0:T(8,128)(2,1)} %get-tuple-element.15), channel_id=1, source_target_pairs={{0,384},{128,256},{256,128},{384,0},{1,385},{129,257},{257,129},{3... | collective-permute-start | bytes 1572872 | tf_op jit(solution)/shard_map/ppermute | solution.py:172
  27.0 0.1 reshape.218
  27.1 0.1 copy.23
  27.2 0.1 mul.124
  27.3 3.0 %all-to-all-done = bf16[32,8,1024]{2,1,0:T(8,128)(2,1)S(1)} async-done(((bf16[32,8,1024]{2,1,0:T(8,128)(2,1)}), bf16[32,8,1024]{2,1,0:T(8,128)(2,1)S(1)}, u32[]{:S(2)}, u32[]{:S(2)}) %all-to-all-start) | async-done | bytes 524320 | tf_op jit(solution)/shard_map/all_to_all | solution.py:26
  30.3 0.6 copy.33
  31.0 10.6 %all-to-all-start.1 = ((bf16[16,8,256]{2,1,0:T(8,128)(2,1)}), bf16[16,8,256]{2,1,0:T(8,128)(2,1)S(1)}, u32[]{:S(2)}, u32[]{:S(2)}) async-start(bf16[16,8,256]{2,1,0:T(8,128)(2,1)} %bitcast.17), calls=%async_computation.1 | async-start | bytes 131072 | tf_op jit(solution)/shard_map/all_to_all | solution.py:26
  41.6 0.6 fusion.7
  42.2 0.1 reshape.219.columns_ref
  42.3 7.1 %all-to-all-done.1.x_ref = bf16[16,8,256]{2,1,0:T(8,128)(2,1)S(1)} async-done(((bf16[16,8,256]{2,1,0:T(8,128)(2,1)}), bf16[16,8,256]{2,1,0:T(8,128)(2,1)S(1)}, u32[]{:S(2)}, u32[]{:S(2)}) %all-to-all-start.1) | async-done | bytes 65568 | tf_op jit(solution)/shard_map/all_to_all | solution.py:26
  49.4 2.8 %shard_map.64 = f32[64,256]{1,0:T(8,128)S(1)} custom-call(s32[16]{0:T(128)S(1)} %copy-done.1, bf16[16,8,256]{2,1,0:T(8,128)(2,1)S(1)} %all-to-all-done.1.x_ref, f32[2,26,1024]{2,1,0:T(8,128)S(1)} %pad_maximum_fusion.1.base_ref, s32[1,1024]{1,0:T(1,128)S(1)} %reshape.219.columns_ref), custom_call_target="tpu_custom_call" | custom-call | tf_op jit(solution)/shard_map/pallas_call | solution.py:133
  52.2 0.7 copy.25
  52.9 4.3 %all-to-all-start.2 = ((f32[64,1,256]{2,1,0:T(1,128)}), f32[64,1,256]{2,1,0:T(1,128)S(1)}, u32[]{:S(2)}, u32[]{:S(2)}) async-start(f32[64,1,256]{2,1,0:T(1,128)} %copy.25), calls=%async_computation.2 | async-start | bytes 131072 | tf_op jit(solution)/shard_map/all_to_all | solution.py:26
  57.2 0.1 dynamic_slice.3.order_ref
  57.3 9.7 %all-to-all-done.2 = f32[64,1,256]{2,1,0:T(1,128)S(1)} async-done(((f32[64,1,256]{2,1,0:T(1,128)}), f32[64,1,256]{2,1,0:T(1,128)S(1)}, u32[]{:S(2)}, u32[]{:S(2)}) %all-to-all-start.2) | async-done | bytes 65568 | tf_op jit(solution)/shard_map/all_to_all | solution.py:26
  67.1 1.1 shard_map.66
  68.2 20.5 %all_to_all.37.sums_ref = bf16[8,32,1024]{2,1,0:T(8,128)(2,1)S(1)} all-to-all(bf16[8,32,1024]{2,1,0:T(8,128)(2,1)S(1)} %shard_map.66), channel_id=1, replica_groups=mesh['x'=4,'z'=8,'order'=16] {'z'}, dimensions={0} | all-to-all | bytes 1048576 | tf_op jit(solution)/shard_map/all_to_all | solution.py:26
  88.7 1.3 %shard_map.67 = f32[32,16,128]{2,1,0:T(8,128)} custom-call(bf16[8,32,1024]{2,1,0:T(8,128)(2,1)S(1)} %all_to_all.37.sums_ref, bf16[256,1024]{1,0:T(8,128)(2,1)S(1)} %bitcast.19), custom_call_target="tpu_custom_call" | custom-call | tf_op jit(solution)/shard_map/pallas_call | solution.py:229
  90.0 10.1 %all-to-all-start.4 = ((f32[512,1,128]{2,1,0:T(1,128)}), f32[512,1,128]{2,1,0:T(1,128)S(1)}, u32[]{:S(2)}, u32[]{:S(2)}) async-start(f32[512,1,128]{2,1,0:T(1,128)} %bitcast.6), calls=%async_computation.4 | async-start | bytes 524288 | tf_op jit(solution)/shard_map/all_to_all | solution.py:26
  100.1 0.2 reshape.222
  100.3 0.3 copy.27
  100.6 0.1 mul.129
  100.7 2.1 %cosine_multiply_fusion = (f32[512,2,1,128]{3,0,2,1:T(8,128)S(1)}, f32[512,2,1,128]{3,0,2,1:T(8,128)S(1)}) fusion(s32[128]{0:T(128)S(1)} %iota_add_fusion, s32[512,2]{0,1:T(2,128)S(1)} %mul.129), kind=kLoop, calls=%fused_computation.10 | loop fusion | flops 2097152 | bytes 1053184 | tf_op jit(solution)/shard_map/mul | solution.py:270
  103.0 0.8 copy.28
  103.8 0.8 reshape.223.table_ref
  104.6 12.5 %all-to-all-done.4 = f32[512,1,128]{2,1,0:T(1,128)S(1)} async-done(((f32[512,1,128]{2,1,0:T(1,128)}), f32[512,1,128]{2,1,0:T(1,128)S(1)}, u32[]{:S(2)}, u32[]{:S(2)}) %all-to-all-start.4) | async-done | bytes 262176 | tf_op jit(solution)/shard_map/all_to_all | solution.py:26
  117.1 1.0 shard_map.68
  (17 shorter events, 0.1 us)
Async XLA Ops:
  0.0 41.6 %copy-start.4 = (s32[26]{0:T(128)S(1)}, s32[26]{0:T(128)}, u32[]{:S(2)}) copy-start(s32[26]{0:T(128)} %constant.58.clone) | copy-start | bytes 316
  0.0 16.0 %copy-start = (bf16[64,16,1024]{2,1,0:T(8,128)(2,1)S(1)}, bf16[64,16,1024]{2,1,0:T(8,128)(2,1)}, u32[]{:S(2)}) copy-start(bf16[64,16,1024]{2,1,0:T(8,128)(2,1)} %param.9) | copy-start | bytes 6291460
  0.0 27.0 %copy-start.3 = (s32[1024]{0:T(1024)S(1)}, s32[1024]{0:T(1024)}, u32[]{:S(2)}) copy-start(s32[1024]{0:T(1024)} %param.8) | copy-start | bytes 12292
  0.0 30.3 %copy-start.2 = (bf16[8,16,256]{2,1,0:T(8,128)(2,1)S(1)}, bf16[8,16,256]{2,1,0:T(8,128)(2,1)}, u32[]{:S(2)}) copy-start(bf16[8,16,256]{2,1,0:T(8,128)(2,1)} %param.6) | copy-start | bytes 196612
  2.1 47.2 %copy-start.1 = (s32[16]{0:T(128)S(1)}, s32[16]{0:T(128)}, u32[]{:S(2)}) copy-start(s32[16]{0:T(128)} %cycle_ref.1) | copy-start | bytes 196
  2.2 28.2 %all-to-all-start = ((bf16[32,8,1024]{2,1,0:T(8,128)(2,1)}), bf16[32,8,1024]{2,1,0:T(8,128)(2,1)S(1)}, u32[]{:S(2)}, u32[]{:S(2)}) async-start(bf16[32,8,1024]{2,1,0:T(8,128)(2,1)} %reshape.217), calls=%async_computation | async-start | bytes 1048576 | tf_op jit(solution)/shard_map/all_to_all | solution.py:26
  17.4 49.6 %collective-permute-start = (bf16[256,1024]{1,0:T(8,128)(2,1)}, bf16[256,1024]{1,0:T(8,128)(2,1)S(1)}, u32[]{:S(2)}, u32[]{:S(2)}) collective-permute-start(bf16[256,1024]{1,0:T(8,128)(2,1)} %get-tuple-element.13), channel_id=1, source_target_pairs={{0,128},{128,0},{256,384},{384,256},{1,129},{129,1},{257,385},{385... | collective-permute-start | bytes 1572872 | tf_op jit(solution)/shard_map/ppermute | solution.py:172
  20.6 46.5 %collective-permute-start.1 = (bf16[256,1024]{1,0:T(8,128)(2,1)}, bf16[256,1024]{1,0:T(8,128)(2,1)S(1)}, u32[]{:S(2)}, u32[]{:S(2)}) collective-permute-start(bf16[256,1024]{1,0:T(8,128)(2,1)} %get-tuple-element.14), channel_id=1, source_target_pairs={{0,256},{128,384},{256,0},{384,128},{1,257},{129,385},{257,1},{385... | collective-permute-start | bytes 1572872 | tf_op jit(solution)/shard_map/ppermute | solution.py:172
  24.9 42.1 %collective-permute-start.2 = (bf16[256,1024]{1,0:T(8,128)(2,1)}, bf16[256,1024]{1,0:T(8,128)(2,1)S(1)}, u32[]{:S(2)}, u32[]{:S(2)}) collective-permute-start(bf16[256,1024]{1,0:T(8,128)(2,1)} %get-tuple-element.15), channel_id=1, source_target_pairs={{0,384},{128,256},{256,128},{384,0},{1,385},{129,257},{257,129},{3... | collective-permute-start | bytes 1572872 | tf_op jit(solution)/shard_map/ppermute | solution.py:172
  31.0 18.4 %all-to-all-start.1 = ((bf16[16,8,256]{2,1,0:T(8,128)(2,1)}), bf16[16,8,256]{2,1,0:T(8,128)(2,1)S(1)}, u32[]{:S(2)}, u32[]{:S(2)}) async-start(bf16[16,8,256]{2,1,0:T(8,128)(2,1)} %bitcast.17), calls=%async_computation.1 | async-start | bytes 131072 | tf_op jit(solution)/shard_map/all_to_all | solution.py:26
  52.9 14.1 %all-to-all-start.2 = ((f32[64,1,256]{2,1,0:T(1,128)}), f32[64,1,256]{2,1,0:T(1,128)S(1)}, u32[]{:S(2)}, u32[]{:S(2)}) async-start(f32[64,1,256]{2,1,0:T(1,128)} %copy.25), calls=%async_computation.2 | async-start | bytes 131072 | tf_op jit(solution)/shard_map/all_to_all | solution.py:26
  90.0 27.1 %all-to-all-start.4 = ((f32[512,1,128]{2,1,0:T(1,128)}), f32[512,1,128]{2,1,0:T(1,128)S(1)}, u32[]{:S(2)}, u32[]{:S(2)}) async-start(f32[512,1,128]{2,1,0:T(1,128)} %bitcast.6), calls=%async_computation.4 | async-start | bytes 524288 | tf_op jit(solution)/shard_map/all_to_all | solution.py:26

commit v4 on v3

--- a/solution.py
+++ b/solution.py
@@ -17,6 +17,8 @@
 RB = 16
 GB = 4
 BLK = ("x", "z")
+ORDER = ("ya", "yb")
+NA, NB = 4, 4
 
 
 BF16, F32 = jnp.bfloat16, jnp.float32
@@ -35,8 +37,10 @@
     return pltpu.CompilerParams(vmem_limit_bytes=mib << 20)
 
 
-def pixel_kernel(cycle_ref, x_ref, base_ref, columns_ref, out_ref, acc_ref, fine_ref, fold_ref):
-    cycle = cycle_ref[lax.axis_index("order")]
+def pixel_kernel(
+    cycle_ref, x_ref, cos_ref, sin_ref, columns_ref, out_ref, acc_ref, fine_ref, fold_ref
+):
+    cycle = cycle_ref[lax.axis_index(ORDER)]
     nearest = jnp.minimum(jnp.minimum(cycle, NSIDE), 4 * NSIDE - cycle)
     rounded, stride = 1, NSIDE
     for index in range(NSIDE.bit_length() - 1):
@@ -71,9 +75,9 @@
         fold_ref[block, 0] = jnp.concatenate(cos_rows, axis=0)
         fold_ref[block, 1] = jnp.concatenate(sin_rows, axis=0)
 
-    c0, s0 = base_ref[0, 18:26, :], base_ref[1, 18:26, :]
+    c0, s0 = cos_ref[18:26, :], sin_ref[18:26, :]
     for b in range(8):
-        c1, s1 = base_ref[0, 10 + b : 11 + b, :], base_ref[1, 10 + b : 11 + b, :]
+        c1, s1 = cos_ref[10 + b : 11 + b, :], sin_ref[10 + b : 11 + b, :]
         fine_ref[0, 8 * b : 8 * b + 8, :] = c1 * c0 - s1 * s0
         fine_ref[1, 8 * b : 8 * b + 8, :] = s1 * c0 + c1 * s0
     acc_ref[...] = jnp.zeros_like(acc_ref)
@@ -83,8 +87,8 @@
         coarse = []
         for a in range(4):
             row0 = pl.ds(2 + block % 2 * 4 + a, 1)
-            c1, s1 = base_ref[0, row1, :], base_ref[1, row1, :]
-            c0, s0 = base_ref[0, row0, :], base_ref[1, row0, :]
+            c1, s1 = cos_ref[row1, :], sin_ref[row1, :]
+            c0, s0 = cos_ref[row0, :], sin_ref[row0, :]
             coarse.append((c1 * c0 - s1 * s0, s1 * c0 + c1 * s0))
         cos_left, sin_left = fold_ref[block, 0], fold_ref[block, 1]
         for tile in range(ORDERS // 256):
@@ -129,12 +133,11 @@
     steps = [512 * a for a in range(2)] + [64 * a for a in range(8)]
     steps = jnp.asarray(steps + [8 * b for b in range(8)] + list(range(8)), jnp.int32)
     angle = (steps[:, None] * columns % NPIX).astype(F32) * (2.0 * math.pi / NPIX)
-    base = jnp.stack([jnp.cos(angle), jnp.sin(angle)])
     return pl.pallas_call(
         pixel_kernel,
         out_shape=jax.ShapeDtypeStruct((64, 256), F32),
         in_specs=[pl.BlockSpec(memory_space=pltpu.SMEM)]
-        + [pl.BlockSpec(memory_space=pltpu.VMEM)] * 3,
+        + [pl.BlockSpec(memory_space=pltpu.VMEM)] * 4,
         out_specs=pl.BlockSpec(memory_space=pltpu.VMEM),
         scratch_shapes=[
             pltpu.VMEM((2, 4 * FIELDS, ORDERS), F32),
@@ -142,7 +145,7 @@
             pltpu.VMEM((4, 2, 4 * FIELDS, 256), BF16),
         ],
         compiler_params=params(8),
-    )(cycle_slot, x, base, columns)
+    )(cycle_slot, x, jnp.cos(angle), jnp.sin(angle), columns)
 
 
 def parts_kernel(healpix_ref, *refs):
@@ -222,85 +225,95 @@
     flipped = own.T
     rows = jnp.concatenate([flipped[g * N_BLK : (g + 1) * N_BLK] for g in range(GB)], axis=1)
     for blk in range(N_BLK):
-        out_ref[blk] = jnp.broadcast_to(rows[blk : blk + 1], (N_ORDER, 128))
+        out_ref[blk] = jnp.broadcast_to(rows[blk : blk + 1], (NA, 128))
 
 
 def analysis(sums, legendre):
     return pl.pallas_call(
         analysis_kernel,
-        out_shape=jax.ShapeDtypeStruct((N_BLK, N_ORDER, 128), F32),
+        out_shape=jax.ShapeDtypeStruct((N_BLK, NA, 128), F32),
         compiler_params=params(8),
     )(sums, legendre)
 
 
-def longitude_kernel(value_ref, table_ref, out_ref):
+def longitude_kernel(value_ref, *refs):
     high, low = split2(value_ref[...])
-    table, rest = split2(table_ref[...])
+    table_refs, out_ref = refs[: 2 * NS], refs[2 * NS]
 
     def product(left, right):
         return lax.dot_general(
             left, right, (((0,), (0,)), ((), ())), preferred_element_type=F32
         )
 
-    sums = product(high, table) + (product(high, rest) + product(low, table))
+    totals = [None] * GB
+    for k, table_ref in enumerate(table_refs):
+        table, rest = split2(table_ref[...])
+        sums = product(high, table) + (product(high, rest) + product(low, table))
+        for g in range(GB):
+            piece = sums[g * 32 + k * 8 : g * 32 + k * 8 + 8]
+            totals[g] = piece if totals[g] is None else totals[g] + piece
     for g in range(GB):
-        total = None
-        for k in range(2 * NS):
-            row = g * 32 + k * 8
-            piece = sums[row : row + 8, k * 128 : k * 128 + 128]
-            total = piece if total is None else total + piece
-        out_ref[:, g, :] = total
-
-
-def longitude_sums(value, table):
+        for b in range(NB):
+            out_ref[b, :, g, :] = totals[g][:, b * 128 : b * 128 + 128]
+
+
+def longitude_sums(value, tables):
     return pl.pallas_call(
         longitude_kernel,
-        out_shape=jax.ShapeDtypeStruct((FIELDS, GB, 128), F32),
-        compiler_params=params(8),
-    )(value, table)
-
-
-def longitude_table(order_slot, order_index):
-    pair = order_slot.reshape(N_ORDER, N_BLK, NS).transpose(1, 0, 2)
-    pair = pair.reshape(ORDERS // NS, NS)
-    longitude = order_index * 128 + jnp.arange(128, dtype=jnp.int32)
-    product = pair[:, :, None] * longitude[None, None, :] % NLON
-    angle = product.astype(F32) * (2.0 * math.pi / NLON)
+        out_shape=jax.ShapeDtypeStruct((NB, FIELDS, GB, 128), F32),
+        compiler_params=params(12),
+    )(value, *tables)
+
+
+def longitude_table(order_slot):
+    own_a, own_b = lax.axis_index("ya"), lax.axis_index("yb")
+    orders = order_slot.reshape(NA, NB, N_BLK, NS)
+    orders = lax.dynamic_index_in_dim(orders, own_b, 1, keepdims=False)
+    orders = orders.transpose(1, 0, 2).reshape(N_BLK * NA, NS)
+    longitude = own_a * (NB * 128) + jnp.arange(NB * 128, dtype=jnp.int32)
     scale = 1.0 / math.sqrt(DEGREES)
-    table = jnp.stack([jnp.cos(angle) * scale, jnp.sin(angle) * -scale], axis=2)
-    return table.reshape(ORDERS // NS, NS * 2 * 128)
+    tables = []
+    for s in range(NS):
+        product = orders[:, s : s + 1] * longitude[None, :] % NLON
+        angle = product.astype(F32) * (2.0 * math.pi / NLON)
+        tables += [jnp.cos(angle) * scale, jnp.sin(angle) * -scale]
+    return tables
 
 
 def local(cotangent, cycle_slot, order_slot, legendre_healpix, legendre_gauss):
-    order_index = lax.axis_index("order")
+    order_index = lax.axis_index(ORDER)
     columns = order_slot.reshape(N_ORDER, NX, SE).transpose(2, 1, 0).reshape(1, ORDERS)
-    lon_table = longitude_table(order_slot, order_index)
     first_slot = order_index * SLOTS + lax.axis_index("x") * SE
     own_orders = lax.dynamic_slice_in_dim(order_slot, first_slot, SE)
 
     parts = exchange_parts(legendre_healpix)
-    gauss = exchange(legendre_gauss.reshape(N_BLK, NS * GB, DEGREES), BLK)
-    gauss, cotangent = lax.optimization_barrier((gauss, cotangent))
-    pixels = exchange(cotangent.transpose(1, 0, 2), "order")
+    gauss = exchange(legendre_gauss, BLK)
+    gauss, cotangent, order_slot = lax.optimization_barrier((gauss, cotangent, order_slot))
+    pixels = exchange(cotangent.transpose(1, 0, 2), ORDER)
+    gauss = gauss.reshape(N_BLK * NS * GB, DEGREES)
+    lon_tables = longitude_table(order_slot)
+    pixels, gauss, lon_tables, own_orders = lax.optimization_barrier(
+        (pixels, gauss, lon_tables, own_orders)
+    )
     fourier = pixel_sums(cycle_slot, pixels, columns)
-    fourier = exchange(fourier, ("x", "order"))
+    fourier = exchange(fourier, ("x",) + ORDER)
     sums = synthesis(own_orders, fourier, parts)
     sums = exchange(sums, "z")
-    gaussian = analysis(sums, gauss.reshape(N_BLK * NS * GB, DEGREES))
-    gathered = exchange(gaussian.reshape(N_BLK * N_ORDER, 128), BLK + ("order",))
-    result = longitude_sums(gathered, lon_table)
-    return result.transpose(2, 0, 1)
+    gaussian = analysis(sums, gauss)
+    gathered = exchange(gaussian.reshape(N_BLK * NA, 128), BLK + ("ya",))
+    result = exchange(longitude_sums(gathered, lon_tables), "yb")
+    return jnp.sum(result, axis=0).transpose(2, 0, 1)
 
 
 def solution(mesh):
-    parts = Mesh(mesh.devices.reshape(NX, NZ, N_ORDER), BLK + ("order",))
+    parts = Mesh(mesh.devices.reshape(NX, NZ, NA, NB), BLK + ORDER)
     placed = (
-        P(None, BLK, "order"),
+        P(None, BLK, ORDER),
         P(BLK),
         P(),
-        P("order", BLK, None),
-        P("order", BLK, None),
+        P(ORDER, BLK, None),
+        P(ORDER, BLK, None),
     )
     return jax.shard_map(
-        local, mesh=parts, in_specs=placed, out_specs=P("order", None, BLK), check_vma=False
-    )
+        local, mesh=parts, in_specs=placed, out_specs=P(ORDER, None, BLK), check_vma=False
+    )

time: 119 us -> 118 us (level)
  blocking collectives: 20.5 us -> 63.4 us
  waiting for transfers between devices: 32.3 us -> 4.64 us
  starting transfers between devices: 48.4 us -> 34.1 us
  local copies, waits for them, and re-layouts: 6.15 us -> 4.5 us
    all_to_all x1 -> x4, blocking collectives: 20.5 us -> 63.4 us  [exchange(): return lax.all_to_all(value, axes, split_axis=0, concat_axis=0, tiled=True)]
    all_to_all x4 -> x2, waiting for transfers between devices: 32.3 us -> 4.63 us  [exchange(): return lax.all_to_all(value, axes, split_axis=0, concat_axis=0, tiled=True)]
    all_to_all x4 -> x2, starting transfers between devices: 38.8 us -> 24.5 us  [exchange(): return lax.all_to_all(value, axes, split_axis=0, concat_axis=0, tiled=True)]
    reshape x3, local copies, waits for them, and re-layouts: 3.17 us -> 1.47 us  [the longest x1 1.16 us: local(): gauss = gauss.reshape(N_BLK * NS * GB, DEGREES)]
    unnamed x11 -> x13, local copies, waits for them, and re-layouts: 0.02 us -> 1.61 us
  transfers between devices with their start and end apart: 7 -> 5, of which waited for: 4 -> 2; matrix products, arithmetic and copies ran while one was open for 6% -> 5% of each run, Pallas kernels for 4% -> 4%
where the time goes in v4:
time: 118 us; the launch traced here: 117 us
  blocking collectives  63.4 us (54%)
  starting transfers between devices  34.1 us (29%)
  Pallas kernels  7.06 us (6%)
  waiting for transfers between devices  4.64 us (4%)
  local copies, waits for them, and re-layouts  4.5 us (4%)
  other arithmetic  3.37 us (3%)
    all_to_all x4, blocking collectives, exchange(): return lax.all_to_all(value, axes, split_axis=0, concat_axis=0, tiled=True)  63.4 us
    all_to_all x2, starting transfers between devices, exchange(): return lax.all_to_all(value, axes, split_axis=0, concat_axis=0, tiled=True)  24.5 us
    ppermute x3, starting transfers between devices, exchange_parts(): result.append(lax.ppermute(parts[k], 'x', [(x, x ^ k) for x in range(NX)]))  9.58 us
    all_to_all x2, waiting for transfers between devices, exchange(): return lax.all_to_all(value, axes, split_axis=0, concat_axis=0, tiled=True)  4.63 us
    pallas_call x1, Pallas kernels, pixel_sums(): pl.pallas_call(pixel_kernel, out_shape=jax.ShapeDtypeStruct((64, 256), F3...  2.86 us
  transfers between devices with their start and end apart: 5, of which 2 were waited for; matrix products, arithmetic and copies ran while one was open for 5% of the time, Pallas kernels for 4%

profile of v4, /device:TPU:1, one launch (start us, length us, event | category | flops | bytes accessed | tf_op | source)
XLA Modules:
  0.0 117.3 jit_solution(8255158263864849251)
XLA Ops:
  0.0 13.9 %all-to-all-start = ((bf16[64,4,1024]{2,1,0:T(4,128)(2,1)}), bf16[64,4,1024]{2,1,0:T(4,128)(2,1)S(1)}, u32[]{:S(2)}, u32[]{:S(2)}) async-start(bf16[64,4,1024]{2,1,0:T(4,128)(2,1)} %param.10), calls=%async_computation | async-start | bytes 1048576 | tf_op jit(solution)/shard_map/all_to_all | solution.py:28
  13.9 1.6 %copy-done = bf16[64,16,1024]{2,1,0:T(8,128)(2,1)S(1)} copy-done((bf16[64,16,1024]{2,1,0:T(8,128)(2,1)S(1)}, bf16[64,16,1024]{2,1,0:T(8,128)(2,1)}, u32[]{:S(2)}) %copy-start) | copy-done | bytes 2097176
  15.5 1.3 %shard_map.65 = (bf16[256,1024]{1,0:T(8,128)(2,1)S(1)}, bf16[256,1024]{1,0:T(8,128)(2,1)}, bf16[256,1024]{1,0:T(8,128)(2,1)}, bf16[256,1024]{1,0:T(8,128)(2,1)}) custom-call(bf16[1024,1024]{1,0:T(8,128)(2,1)S(1)} %bitcast.23), custom_call_target="tpu_custom_call" | custom-call | tf_op jit(solution)/shard_map/pallas_call | solution.py:165
  16.8 3.1 %collective-permute-start = (bf16[256,1024]{1,0:T(8,128)(2,1)}, bf16[256,1024]{1,0:T(8,128)(2,1)S(1)}, u32[]{:S(2)}, u32[]{:S(2)}) collective-permute-start(bf16[256,1024]{1,0:T(8,128)(2,1)} %get-tuple-element.25), channel_id=1, source_target_pairs={{0,128},{128,0},{256,384},{384,256},{1,129},{129,1},{257,385},{385... | collective-permute-start | bytes 1572872 | tf_op jit(solution)/shard_map/ppermute | solution.py:175
  20.0 4.3 %collective-permute-start.1 = (bf16[256,1024]{1,0:T(8,128)(2,1)}, bf16[256,1024]{1,0:T(8,128)(2,1)S(1)}, u32[]{:S(2)}, u32[]{:S(2)}) collective-permute-start(bf16[256,1024]{1,0:T(8,128)(2,1)} %get-tuple-element.26), channel_id=1, source_target_pairs={{0,256},{128,384},{256,0},{384,128},{1,257},{129,385},{257,1},{385... | collective-permute-start | bytes 1572872 | tf_op jit(solution)/shard_map/ppermute | solution.py:175
  24.3 2.1 %collective-permute-start.2 = (bf16[256,1024]{1,0:T(8,128)(2,1)}, bf16[256,1024]{1,0:T(8,128)(2,1)}, u32[]{:S(2)}, u32[]{:S(2)}) collective-permute-start(bf16[256,1024]{1,0:T(8,128)(2,1)} %get-tuple-element.27), channel_id=1, source_target_pairs={{0,384},{128,256},{256,128},{384,0},{1,385},{129,257},{257,129},{3... | collective-permute-start | bytes 1572872 | tf_op jit(solution)/shard_map/ppermute | solution.py:175
  26.4 0.1 reshape.33
  26.5 0.1 copy.18
  26.6 0.1 reshape.34.columns_ref
  26.7 0.1 mul.97
  26.8 0.1 dynamic_slice.8.order_ref
  26.9 0.6 fusion.9
  27.5 0.7 all-to-all-done
  28.2 0.7 copy.26
  28.9 10.6 %all-to-all-start.1 = ((bf16[16,8,256]{2,1,0:T(8,128)(2,1)}), bf16[16,8,256]{2,1,0:T(8,128)(2,1)S(1)}, u32[]{:S(2)}, u32[]{:S(2)}) async-start(bf16[16,8,256]{2,1,0:T(8,128)(2,1)} %bitcast.22), calls=%async_computation.1 | async-start | bytes 131072 | tf_op jit(solution)/shard_map/all_to_all | solution.py:28
  39.5 0.2 reshape.31
  39.8 0.1 copy.16
  39.8 0.1 copy.17
  39.9 0.1 reshape.32
  40.1 2.2 %sine_multiply_fusion = (f32[128,512]{1,0:T(8,128)S(1)}, f32[128,512]{1,0:T(8,128)S(1)}, f32[128,512]{1,0:T(8,128)S(1)}, f32[128,512]{1,0:T(8,128)S(1)}) fusion(s32[512]{0:T(512)S(1)} %iota_add_fusion, s32[128]{0:T(128)S(1)} %get-tuple-element.41, s32[128]{0:T(128)S(1)} %get-tuple-element.42), kind=kLoop, calls=%fused_computation.16 | loop fusion | flops 2097152 | bytes 1051648 | tf_op jit(solution)/shard_map/mul | solution.py:279
  42.2 1.2 reshape.30.legendre_ref
  43.4 3.9 %all-to-all-done.1.x_ref = bf16[16,8,256]{2,1,0:T(8,128)(2,1)S(1)} async-done(((bf16[16,8,256]{2,1,0:T(8,128)(2,1)}), bf16[16,8,256]{2,1,0:T(8,128)(2,1)S(1)}, u32[]{:S(2)}, u32[]{:S(2)}) %all-to-all-start.1) | async-done | bytes 65568 | tf_op jit(solution)/shard_map/all_to_all | solution.py:28
  47.3 2.9 %shard_map.64 = f32[64,256]{1,0:T(8,128)S(1)} custom-call(s32[16]{0:T(128)S(1)} %copy-done.1, bf16[16,8,256]{2,1,0:T(8,128)(2,1)S(1)} %all-to-all-done.1.x_ref, f32[26,1024]{1,0:T(8,128)S(1)} %get-tuple-element.34.cos_ref, f32[26,1024]{1,0:T(8,128)S(1)} %get-tuple-element.33.sin_ref, s32[1,1024]{1,0:T(1,128)S(1)} %reshape.34.columns_ref), custom_call_target="tpu_custom_call" | custom-call | tf_op jit(solution)/shard_map/pallas_call | solution.py:136
  50.2 0.1 copy.20
  50.3 14.6 %all_to_all.42 = f32[64,1,256]{2,1,0:T(1,128)S(1)} all-to-all(f32[64,1,256]{2,1,0:T(1,128)S(1)} %copy.20), channel_id=1, replica_groups=mesh['x'=4,'z'=8,'ya'=4,'yb'=4] {'x','ya','yb'}, dimensions={0} | all-to-all | bytes 131072 | tf_op jit(solution)/shard_map/all_to_all | solution.py:28
  64.9 1.6 %shard_map.66 = bf16[8,32,1024]{2,1,0:T(8,128)(2,1)S(1)} custom-call(s32[16]{0:T(128)S(1)} %dynamic_slice.8.order_ref, f32[64,256]{1,0:T(8,128)S(1)} %bitcast.24, bf16[256,1024]{1,0:T(8,128)(2,1)S(1)} %get-tuple-element.24.refs_0_, bf16[256,1024]{1,0:T(8,128)(2,1)S(1)} %collective-permute-done.refs_1_, bf16[256,1024]{1,0:T(8,128)(2,1)S(1)} %collective-permute-done.1.refs_2_, ...), custom_call_target="tpu_custom_call" | custom-call | tf_op jit(solution)/shard_map/pallas_call | solution.py:196
  66.6 21.7 %all_to_all.43.sums_ref = bf16[8,32,1024]{2,1,0:T(8,128)(2,1)S(1)} all-to-all(bf16[8,32,1024]{2,1,0:T(8,128)(2,1)S(1)} %shard_map.66), channel_id=1, replica_groups=mesh['x'=4,'z'=8,'ya'=4,'yb'=4] {'z'}, dimensions={0} | all-to-all | bytes 1048576 | tf_op jit(solution)/shard_map/all_to_all | solution.py:28
  88.3 0.6 shard_map.67
  88.9 18.5 %all_to_all.44 = f32[128,1,128]{2,1,0:T(1,128)S(1)} all-to-all(f32[128,1,128]{2,1,0:T(1,128)S(1)} %bitcast.27), channel_id=1, replica_groups=mesh['x'=4,'z'=8,'ya'=4,'yb'=4] {'x','z','ya'}, dimensions={0} | all-to-all | bytes 131072 | tf_op jit(solution)/shard_map/all_to_all | solution.py:28
  107.4 0.6 shard_map.68
  108.0 8.6 %all_to_all.45 = f32[4,8,4,128]{3,2,1,0:T(4,128)S(1)} all-to-all(f32[4,8,4,128]{3,2,1,0:T(4,128)S(1)} %shard_map.68), channel_id=1, replica_groups=mesh['x'=4,'z'=8,'ya'=4,'yb'=4] {'yb'}, dimensions={0} | all-to-all | bytes 131072 | tf_op jit(solution)/shard_map/all_to_all | solution.py:28
  116.6 0.6 reduce_sum.9
  (18 shorter events, 0.1 us)
Async XLA Ops:
  0.0 26.9 %copy-start.5 = (s32[26]{0:T(128)S(1)}, s32[26]{0:T(128)}, u32[]{:S(2)}) copy-start(s32[26]{0:T(128)} %constant.72.clone) | copy-start | bytes 316
  0.0 26.4 %copy-start.4 = (s32[1024]{0:T(1024)S(1)}, s32[1024]{0:T(1024)}, u32[]{:S(2)}) copy-start(s32[1024]{0:T(1024)} %param.8) | copy-start | bytes 12292
  0.0 28.2 %copy-start.3 = (bf16[8,16,256]{2,1,0:T(8,128)(2,1)S(1)}, bf16[8,16,256]{2,1,0:T(8,128)(2,1)}, u32[]{:S(2)}) copy-start(bf16[8,16,256]{2,1,0:T(8,128)(2,1)} %param.6) | copy-start | bytes 196612
  0.0 28.2 %all-to-all-start = ((bf16[64,4,1024]{2,1,0:T(4,128)(2,1)}), bf16[64,4,1024]{2,1,0:T(4,128)(2,1)S(1)}, u32[]{:S(2)}, u32[]{:S(2)}) async-start(bf16[64,4,1024]{2,1,0:T(4,128)(2,1)} %param.10), calls=%async_computation | async-start | bytes 1048576 | tf_op jit(solution)/shard_map/all_to_all | solution.py:28
  13.9 1.6 %copy-start = (bf16[64,16,1024]{2,1,0:T(8,128)(2,1)S(1)}, bf16[64,16,1024]{2,1,0:T(8,128)(2,1)}, u32[]{:S(2)}) copy-start(bf16[64,16,1024]{2,1,0:T(8,128)(2,1)} %param.9) | copy-start | bytes 6291460
  16.8 30.5 %copy-start.1 = (s32[16]{0:T(128)S(1)}, s32[16]{0:T(128)}, u32[]{:S(2)}) copy-start(s32[16]{0:T(128)} %cycle_ref.1) | copy-start | bytes 196
  16.8 48.1 %collective-permute-start = (bf16[256,1024]{1,0:T(8,128)(2,1)}, bf16[256,1024]{1,0:T(8,128)(2,1)S(1)}, u32[]{:S(2)}, u32[]{:S(2)}) collective-permute-start(bf16[256,1024]{1,0:T(8,128)(2,1)} %get-tuple-element.25), channel_id=1, source_target_pairs={{0,128},{128,0},{256,384},{384,256},{1,129},{129,1},{257,385},{385... | collective-permute-start | bytes 1572872 | tf_op jit(solution)/shard_map/ppermute | solution.py:175
  20.0 44.9 %collective-permute-start.1 = (bf16[256,1024]{1,0:T(8,128)(2,1)}, bf16[256,1024]{1,0:T(8,128)(2,1)S(1)}, u32[]{:S(2)}, u32[]{:S(2)}) collective-permute-start(bf16[256,1024]{1,0:T(8,128)(2,1)} %get-tuple-element.26), channel_id=1, source_target_pairs={{0,256},{128,384},{256,0},{384,128},{1,257},{129,385},{257,1},{385... | collective-permute-start | bytes 1572872 | tf_op jit(solution)/shard_map/ppermute | solution.py:175
  24.3 40.6 %collective-permute-start.2 = (bf16[256,1024]{1,0:T(8,128)(2,1)}, bf16[256,1024]{1,0:T(8,128)(2,1)}, u32[]{:S(2)}, u32[]{:S(2)}) collective-permute-start(bf16[256,1024]{1,0:T(8,128)(2,1)} %get-tuple-element.27), channel_id=1, source_target_pairs={{0,384},{128,256},{256,128},{384,0},{1,385},{129,257},{257,129},{3... | collective-permute-start | bytes 1572872 | tf_op jit(solution)/shard_map/ppermute | solution.py:175
  28.2 11.9 %copy-start.2 = (bf16[64,4,1024]{2,1,0:T(4,128)(2,1)}, bf16[64,4,1024]{2,1,0:T(4,128)(2,1)S(1)}, u32[]{:S(2)}) copy-start(bf16[64,4,1024]{2,1,0:T(4,128)(2,1)S(1)} %all-to-all-done) | copy-start | bytes 1572868
  28.9 18.4 %all-to-all-start.1 = ((bf16[16,8,256]{2,1,0:T(8,128)(2,1)}), bf16[16,8,256]{2,1,0:T(8,128)(2,1)S(1)}, u32[]{:S(2)}, u32[]{:S(2)}) async-start(bf16[16,8,256]{2,1,0:T(8,128)(2,1)} %bitcast.22), calls=%async_computation.1 | async-start | bytes 131072 | tf_op jit(solution)/shard_map/all_to_all | solution.py:28

commit v5 on v4

--- a/solution.py
+++ b/solution.py
@@ -224,14 +224,14 @@
     own = jnp.concatenate([value[:16, :128], value[16:, 128:]], axis=0)
     flipped = own.T
     rows = jnp.concatenate([flipped[g * N_BLK : (g + 1) * N_BLK] for g in range(GB)], axis=1)
-    for blk in range(N_BLK):
-        out_ref[blk] = jnp.broadcast_to(rows[blk : blk + 1], (NA, 128))
+    for a in range(NA):
+        out_ref[a] = rows
 
 
 def analysis(sums, legendre):
     return pl.pallas_call(
         analysis_kernel,
-        out_shape=jax.ShapeDtypeStruct((N_BLK, NA, 128), F32),
+        out_shape=jax.ShapeDtypeStruct((NA, N_BLK, 128), F32),
         compiler_params=params(8),
     )(sums, legendre)
 
@@ -266,11 +266,11 @@
 
 
 def longitude_table(order_slot):
-    own_a, own_b = lax.axis_index("ya"), lax.axis_index("yb")
     orders = order_slot.reshape(NA, NB, N_BLK, NS)
-    orders = lax.dynamic_index_in_dim(orders, own_b, 1, keepdims=False)
-    orders = orders.transpose(1, 0, 2).reshape(N_BLK * NA, NS)
-    longitude = own_a * (NB * 128) + jnp.arange(NB * 128, dtype=jnp.int32)
+    orders = lax.dynamic_index_in_dim(orders, lax.axis_index("ya"), 0, keepdims=False)
+    orders = orders.reshape(NB * N_BLK, NS)
+    column = jnp.arange(NA * 128, dtype=jnp.int32)
+    longitude = (column // 128 * NB + lax.axis_index("yb")) * 128 + column % 128
     scale = 1.0 / math.sqrt(DEGREES)
     tables = []
     for s in range(NS):
@@ -300,8 +300,8 @@
     sums = synthesis(own_orders, fourier, parts)
     sums = exchange(sums, "z")
     gaussian = analysis(sums, gauss)
-    gathered = exchange(gaussian.reshape(N_BLK * NA, 128), BLK + ("ya",))
-    result = exchange(longitude_sums(gathered, lon_tables), "yb")
+    gathered = exchange(gaussian.reshape(NA * N_BLK, 128), ("yb",) + BLK)
+    result = exchange(longitude_sums(gathered, lon_tables), "ya")
     return jnp.sum(result, axis=0).transpose(2, 0, 1)
 
 

time: 118 us -> 117 us (level)
  no operation moved by 1% of the time
where the time goes in v5:
time: 117 us; the launch traced here: 116 us
  blocking collectives  62.4 us (53%)
  starting transfers between devices  34.1 us (29%)
  Pallas kernels  7.04 us (6%)
  waiting for transfers between devices  4.71 us (4%)
  local copies, waits for them, and re-layouts  4.42 us (4%)
  other arithmetic  3.4 us (3%)
    all_to_all x4, blocking collectives, exchange(): return lax.all_to_all(value, axes, split_axis=0, concat_axis=0, tiled=True)  62.4 us
    all_to_all x2, starting transfers between devices, exchange(): return lax.all_to_all(value, axes, split_axis=0, concat_axis=0, tiled=True)  24.5 us
    ppermute x3, starting transfers between devices, exchange_parts(): result.append(lax.ppermute(parts[k], 'x', [(x, x ^ k) for x in range(NX)]))  9.58 us
    all_to_all x2, waiting for transfers between devices, exchange(): return lax.all_to_all(value, axes, split_axis=0, concat_axis=0, tiled=True)  4.7 us
    pallas_call x1, Pallas kernels, pixel_sums(): pl.pallas_call(pixel_kernel, out_shape=jax.ShapeDtypeStruct((64, 256), F3...  2.84 us
  transfers between devices with their start and end apart: 5, of which 2 were waited for; matrix products, arithmetic and copies ran while one was open for 5% of the time, Pallas kernels for 4%

profile of v5, /device:TPU:1, one launch (start us, length us, event | category | flops | bytes accessed | tf_op | source)
XLA Modules:
  0.0 116.2 jit_solution(10681907647878405295)
XLA Ops:
  0.0 13.9 %all-to-all-start = ((bf16[64,4,1024]{2,1,0:T(4,128)(2,1)}), bf16[64,4,1024]{2,1,0:T(4,128)(2,1)S(1)}, u32[]{:S(2)}, u32[]{:S(2)}) async-start(bf16[64,4,1024]{2,1,0:T(4,128)(2,1)} %param.10), calls=%async_computation | async-start | bytes 1048576 | tf_op jit(solution)/shard_map/all_to_all | solution.py:28
  13.9 1.6 %copy-done = bf16[64,16,1024]{2,1,0:T(8,128)(2,1)S(1)} copy-done((bf16[64,16,1024]{2,1,0:T(8,128)(2,1)S(1)}, bf16[64,16,1024]{2,1,0:T(8,128)(2,1)}, u32[]{:S(2)}) %copy-start) | copy-done | bytes 2097176
  15.5 1.3 %shard_map.65 = (bf16[256,1024]{1,0:T(8,128)(2,1)S(1)}, bf16[256,1024]{1,0:T(8,128)(2,1)}, bf16[256,1024]{1,0:T(8,128)(2,1)}, bf16[256,1024]{1,0:T(8,128)(2,1)}) custom-call(bf16[1024,1024]{1,0:T(8,128)(2,1)S(1)} %bitcast.17), custom_call_target="tpu_custom_call" | custom-call | tf_op jit(solution)/shard_map/pallas_call | solution.py:165
  16.8 3.1 %collective-permute-start = (bf16[256,1024]{1,0:T(8,128)(2,1)}, bf16[256,1024]{1,0:T(8,128)(2,1)S(1)}, u32[]{:S(2)}, u32[]{:S(2)}) collective-permute-start(bf16[256,1024]{1,0:T(8,128)(2,1)} %get-tuple-element.25), channel_id=1, source_target_pairs={{0,128},{128,0},{256,384},{384,256},{1,129},{129,1},{257,385},{385... | collective-permute-start | bytes 1572872 | tf_op jit(solution)/shard_map/ppermute | solution.py:175
  20.0 4.3 %collective-permute-start.1 = (bf16[256,1024]{1,0:T(8,128)(2,1)}, bf16[256,1024]{1,0:T(8,128)(2,1)S(1)}, u32[]{:S(2)}, u32[]{:S(2)}) collective-permute-start(bf16[256,1024]{1,0:T(8,128)(2,1)} %get-tuple-element.26), channel_id=1, source_target_pairs={{0,256},{128,384},{256,0},{384,128},{1,257},{129,385},{257,1},{385... | collective-permute-start | bytes 1572872 | tf_op jit(solution)/shard_map/ppermute | solution.py:175
  24.3 2.1 %collective-permute-start.2 = (bf16[256,1024]{1,0:T(8,128)(2,1)}, bf16[256,1024]{1,0:T(8,128)(2,1)}, u32[]{:S(2)}, u32[]{:S(2)}) collective-permute-start(bf16[256,1024]{1,0:T(8,128)(2,1)} %get-tuple-element.27), channel_id=1, source_target_pairs={{0,384},{128,256},{256,128},{384,0},{1,385},{129,257},{257,129},{3... | collective-permute-start | bytes 1572872 | tf_op jit(solution)/shard_map/ppermute | solution.py:175
  26.4 0.1 reshape.54
  26.5 0.1 copy.16
  26.6 0.1 reshape.55.columns_ref
  26.7 0.1 mul.114
  26.8 0.1 dynamic_slice.8.order_ref
  26.9 0.6 fusion.9
  27.5 0.7 all-to-all-done
  28.2 0.7 copy.27
  28.9 10.6 %all-to-all-start.1 = ((bf16[16,8,256]{2,1,0:T(8,128)(2,1)}), bf16[16,8,256]{2,1,0:T(8,128)(2,1)S(1)}, u32[]{:S(2)}, u32[]{:S(2)}) async-start(bf16[16,8,256]{2,1,0:T(8,128)(2,1)} %bitcast.16), calls=%async_computation.1 | async-start | bytes 131072 | tf_op jit(solution)/shard_map/all_to_all | solution.py:28
  39.5 0.2 reshape.52
  39.8 0.1 fusion.22
  39.8 0.1 copy.23
  39.9 0.1 copy.22
  40.0 2.2 %sine_multiply_fusion = (f32[128,512]{1,0:T(8,128)S(1)}, f32[128,512]{1,0:T(8,128)S(1)}, f32[128,512]{1,0:T(8,128)S(1)}, f32[128,512]{1,0:T(8,128)S(1)}) fusion(s32[512]{0:T(512)S(1)} %fusion.18, s32[128]{0:T(128)S(1)} %bitcast.24, s32[128]{0:T(128)S(1)} %bitcast.25), kind=kLoop, calls=%fused_computation.16 | loop fusion | flops 2097152 | bytes 1051648 | tf_op jit(solution)/shard_map/mul | solution.py:279
  42.2 1.2 %reshape.51.legendre_ref = bf16[256,1024]{1,0:T(8,128)(2,1)S(1)} reshape(bf16[64,4,1024]{2,1,0:T(4,128)(2,1)} %copy-done.2) | data formatting | bytes 1048576 | tf_op jit(solution)/shard_map/reshape | solution.py:293
  43.3 4.0 %all-to-all-done.1.x_ref = bf16[16,8,256]{2,1,0:T(8,128)(2,1)S(1)} async-done(((bf16[16,8,256]{2,1,0:T(8,128)(2,1)}), bf16[16,8,256]{2,1,0:T(8,128)(2,1)S(1)}, u32[]{:S(2)}, u32[]{:S(2)}) %all-to-all-start.1) | async-done | bytes 65568 | tf_op jit(solution)/shard_map/all_to_all | solution.py:28
  47.3 2.8 %shard_map.64 = f32[64,256]{1,0:T(8,128)S(1)} custom-call(s32[16]{0:T(128)S(1)} %copy-done.1, bf16[16,8,256]{2,1,0:T(8,128)(2,1)S(1)} %all-to-all-done.1.x_ref, f32[26,1024]{1,0:T(8,128)S(1)} %get-tuple-element.36.cos_ref, f32[26,1024]{1,0:T(8,128)S(1)} %get-tuple-element.35.sin_ref, s32[1,1024]{1,0:T(1,128)S(1)} %reshape.55.columns_ref), custom_call_target="tpu_custom_call" | custom-call | tf_op jit(solution)/shard_map/pallas_call | solution.py:136
  50.2 0.1 copy.18
  50.3 14.5 %all_to_all.42 = f32[64,1,256]{2,1,0:T(1,128)S(1)} all-to-all(f32[64,1,256]{2,1,0:T(1,128)S(1)} %copy.18), channel_id=1, replica_groups=mesh['x'=4,'z'=8,'ya'=4,'yb'=4] {'x','ya','yb'}, dimensions={0} | all-to-all | bytes 131072 | tf_op jit(solution)/shard_map/all_to_all | solution.py:28
  64.8 1.6 %shard_map.66 = bf16[8,32,1024]{2,1,0:T(8,128)(2,1)S(1)} custom-call(s32[16]{0:T(128)S(1)} %dynamic_slice.8.order_ref, f32[64,256]{1,0:T(8,128)S(1)} %bitcast.18, bf16[256,1024]{1,0:T(8,128)(2,1)S(1)} %get-tuple-element.24.refs_0_, bf16[256,1024]{1,0:T(8,128)(2,1)S(1)} %collective-permute-done.refs_1_, bf16[256,1024]{1,0:T(8,128)(2,1)S(1)} %collective-permute-done.1.refs_2_, ...), custom_call_target="tpu_custom_call" | custom-call | tf_op jit(solution)/shard_map/pallas_call | solution.py:196
  66.5 21.7 %all_to_all.43.sums_ref = bf16[8,32,1024]{2,1,0:T(8,128)(2,1)S(1)} all-to-all(bf16[8,32,1024]{2,1,0:T(8,128)(2,1)S(1)} %shard_map.66), channel_id=1, replica_groups=mesh['x'=4,'z'=8,'ya'=4,'yb'=4] {'z'}, dimensions={0} | all-to-all | bytes 1048576 | tf_op jit(solution)/shard_map/all_to_all | solution.py:28
  88.2 0.6 shard_map.67
  88.8 16.9 %all_to_all.44 = f32[128,1,128]{2,1,0:T(1,128)S(1)} all-to-all(f32[128,1,128]{2,1,0:T(1,128)S(1)} %bitcast.21), channel_id=1, replica_groups=mesh['x'=4,'z'=8,'ya'=4,'yb'=4] {'yb','x','z'}, dimensions={0} | all-to-all | bytes 131072 | tf_op jit(solution)/shard_map/all_to_all | solution.py:28
  105.7 0.6 shard_map.68
  106.3 9.3 %all_to_all.45 = f32[4,8,4,128]{3,2,1,0:T(4,128)S(1)} all-to-all(f32[4,8,4,128]{3,2,1,0:T(4,128)S(1)} %shard_map.68), channel_id=1, replica_groups=mesh['x'=4,'z'=8,'ya'=4,'yb'=4] {'ya'}, dimensions={0} | all-to-all | bytes 131072 | tf_op jit(solution)/shard_map/all_to_all | solution.py:28
  115.6 0.6 reduce_sum.9
  (17 shorter events, 0.1 us)
Async XLA Ops:
  0.0 26.9 %copy-start.5 = (s32[26]{0:T(128)S(1)}, s32[26]{0:T(128)}, u32[]{:S(2)}) copy-start(s32[26]{0:T(128)} %constant.102.clone) | copy-start | bytes 316
  0.0 26.4 %copy-start.4 = (s32[1024]{0:T(1024)S(1)}, s32[1024]{0:T(1024)}, u32[]{:S(2)}) copy-start(s32[1024]{0:T(1024)} %param.8) | copy-start | bytes 12292
  0.0 28.2 %copy-start.3 = (bf16[8,16,256]{2,1,0:T(8,128)(2,1)S(1)}, bf16[8,16,256]{2,1,0:T(8,128)(2,1)}, u32[]{:S(2)}) copy-start(bf16[8,16,256]{2,1,0:T(8,128)(2,1)} %param.6) | copy-start | bytes 196612
  0.0 28.2 %all-to-all-start = ((bf16[64,4,1024]{2,1,0:T(4,128)(2,1)}), bf16[64,4,1024]{2,1,0:T(4,128)(2,1)S(1)}, u32[]{:S(2)}, u32[]{:S(2)}) async-start(bf16[64,4,1024]{2,1,0:T(4,128)(2,1)} %param.10), calls=%async_computation | async-start | bytes 1048576 | tf_op jit(solution)/shard_map/all_to_all | solution.py:28
  13.9 1.6 %copy-start = (bf16[64,16,1024]{2,1,0:T(8,128)(2,1)S(1)}, bf16[64,16,1024]{2,1,0:T(8,128)(2,1)}, u32[]{:S(2)}) copy-start(bf16[64,16,1024]{2,1,0:T(8,128)(2,1)} %param.9) | copy-start | bytes 6291460
  16.8 30.5 %copy-start.1 = (s32[16]{0:T(128)S(1)}, s32[16]{0:T(128)}, u32[]{:S(2)}) copy-start(s32[16]{0:T(128)} %cycle_ref.1) | copy-start | bytes 196
  16.8 48.0 %collective-permute-start = (bf16[256,1024]{1,0:T(8,128)(2,1)}, bf16[256,1024]{1,0:T(8,128)(2,1)S(1)}, u32[]{:S(2)}, u32[]{:S(2)}) collective-permute-start(bf16[256,1024]{1,0:T(8,128)(2,1)} %get-tuple-element.25), channel_id=1, source_target_pairs={{0,128},{128,0},{256,384},{384,256},{1,129},{129,1},{257,385},{385... | collective-permute-start | bytes 1572872 | tf_op jit(solution)/shard_map/ppermute | solution.py:175
  20.0 44.8 %collective-permute-start.1 = (bf16[256,1024]{1,0:T(8,128)(2,1)}, bf16[256,1024]{1,0:T(8,128)(2,1)S(1)}, u32[]{:S(2)}, u32[]{:S(2)}) collective-permute-start(bf16[256,1024]{1,0:T(8,128)(2,1)} %get-tuple-element.26), channel_id=1, source_target_pairs={{0,256},{128,384},{256,0},{384,128},{1,257},{129,385},{257,1},{385... | collective-permute-start | bytes 1572872 | tf_op jit(solution)/shard_map/ppermute | solution.py:175
  24.3 40.5 %collective-permute-start.2 = (bf16[256,1024]{1,0:T(8,128)(2,1)}, bf16[256,1024]{1,0:T(8,128)(2,1)}, u32[]{:S(2)}, u32[]{:S(2)}) collective-permute-start(bf16[256,1024]{1,0:T(8,128)(2,1)} %get-tuple-element.27), channel_id=1, source_target_pairs={{0,384},{128,256},{256,128},{384,0},{1,385},{129,257},{257,129},{3... | collective-permute-start | bytes 1572872 | tf_op jit(solution)/shard_map/ppermute | solution.py:175
  28.2 11.8 %copy-start.2 = (bf16[64,4,1024]{2,1,0:T(4,128)(2,1)}, bf16[64,4,1024]{2,1,0:T(4,128)(2,1)S(1)}, u32[]{:S(2)}) copy-start(bf16[64,4,1024]{2,1,0:T(4,128)(2,1)S(1)} %all-to-all-done) | copy-start | bytes 1572868
  28.9 18.4 %all-to-all-start.1 = ((bf16[16,8,256]{2,1,0:T(8,128)(2,1)}), bf16[16,8,256]{2,1,0:T(8,128)(2,1)S(1)}, u32[]{:S(2)}, u32[]{:S(2)}) async-start(bf16[16,8,256]{2,1,0:T(8,128)(2,1)} %bitcast.16), calls=%async_computation.1 | async-start | bytes 131072 | tf_op jit(solution)/shard_map/all_to_all | solution.py:28

commit v6 on v5

--- a/solution.py
+++ b/solution.py
@@ -18,7 +18,7 @@
 GB = 4
 BLK = ("x", "z")
 ORDER = ("ya", "yb")
-NA, NB = 4, 4
+NA, NB = 8, 2
 
 
 BF16, F32 = jnp.bfloat16, jnp.float32
@@ -224,14 +224,14 @@
     own = jnp.concatenate([value[:16, :128], value[16:, 128:]], axis=0)
     flipped = own.T
     rows = jnp.concatenate([flipped[g * N_BLK : (g + 1) * N_BLK] for g in range(GB)], axis=1)
-    for a in range(NA):
-        out_ref[a] = rows
+    for b in range(NB):
+        out_ref[b] = rows
 
 
 def analysis(sums, legendre):
     return pl.pallas_call(
         analysis_kernel,
-        out_shape=jax.ShapeDtypeStruct((NA, N_BLK, 128), F32),
+        out_shape=jax.ShapeDtypeStruct((NB, N_BLK, 128), F32),
         compiler_params=params(8),
     )(sums, legendre)
 
@@ -253,14 +253,14 @@
             piece = sums[g * 32 + k * 8 : g * 32 + k * 8 + 8]
             totals[g] = piece if totals[g] is None else totals[g] + piece
     for g in range(GB):
-        for b in range(NB):
-            out_ref[b, :, g, :] = totals[g][:, b * 128 : b * 128 + 128]
+        for a in range(NA):
+            out_ref[a, :, g, :] = totals[g][:, a * 128 : a * 128 + 128]
 
 
 def longitude_sums(value, tables):
     return pl.pallas_call(
         longitude_kernel,
-        out_shape=jax.ShapeDtypeStruct((NB, FIELDS, GB, 128), F32),
+        out_shape=jax.ShapeDtypeStruct((NA, FIELDS, GB, 128), F32),
         compiler_params=params(12),
     )(value, *tables)
 
@@ -300,7 +300,7 @@
     sums = synthesis(own_orders, fourier, parts)
     sums = exchange(sums, "z")
     gaussian = analysis(sums, gauss)
-    gathered = exchange(gaussian.reshape(NA * N_BLK, 128), ("yb",) + BLK)
+    gathered = exchange(gaussian.reshape(NB * N_BLK, 128), ("yb",) + BLK)
     result = exchange(longitude_sums(gathered, lon_tables), "ya")
     return jnp.sum(result, axis=0).transpose(2, 0, 1)
 

time: 117 us -> 116 us (level)
  blocking collectives: 62.4 us -> 60.7 us
    all_to_all x4, blocking collectives: 62.4 us -> 60.7 us  [exchange(): return lax.all_to_all(value, axes, split_axis=0, concat_axis=0, tiled=True)]
where the time goes in v6:
time: 116 us; the launch traced here: 115 us
  blocking collectives  60.7 us (52%)
  starting transfers between devices  34.1 us (29%)
  Pallas kernels  7.44 us (6%)
  waiting for transfers between devices  4.73 us (4%)
  local copies, waits for them, and re-layouts  4.41 us (4%)
  other arithmetic  3.4 us (3%)
    all_to_all x4, blocking collectives, exchange(): return lax.all_to_all(value, axes, split_axis=0, concat_axis=0, tiled=True)  60.7 us
    all_to_all x2, starting transfers between devices, exchange(): return lax.all_to_all(value, axes, split_axis=0, concat_axis=0, tiled=True)  24.5 us
    ppermute x3, starting transfers between devices, exchange_parts(): result.append(lax.ppermute(parts[k], 'x', [(x, x ^ k) for x in range(NX)]))  9.58 us
    all_to_all x2, waiting for transfers between devices, exchange(): return lax.all_to_all(value, axes, split_axis=0, concat_axis=0, tiled=True)  4.72 us
    pallas_call x1, Pallas kernels, pixel_sums(): pl.pallas_call(pixel_kernel, out_shape=jax.ShapeDtypeStruct((64, 256), F3...  2.84 us
  transfers between devices with their start and end apart: 5, of which 2 were waited for; matrix products, arithmetic and copies ran while one was open for 5% of the time, Pallas kernels for 4%

profile of v6, /device:TPU:1, one launch (start us, length us, event | category | flops | bytes accessed | tf_op | source)
XLA Modules:
  0.0 114.9 jit_solution(3622136160733826512)
XLA Ops:
  0.0 13.9 %all-to-all-start = ((bf16[64,4,1024]{2,1,0:T(4,128)(2,1)}), bf16[64,4,1024]{2,1,0:T(4,128)(2,1)S(1)}, u32[]{:S(2)}, u32[]{:S(2)}) async-start(bf16[64,4,1024]{2,1,0:T(4,128)(2,1)} %param.10), calls=%async_computation | async-start | bytes 1048576 | tf_op jit(solution)/shard_map/all_to_all | solution.py:28
  13.9 1.6 %copy-done = bf16[64,16,1024]{2,1,0:T(8,128)(2,1)S(1)} copy-done((bf16[64,16,1024]{2,1,0:T(8,128)(2,1)S(1)}, bf16[64,16,1024]{2,1,0:T(8,128)(2,1)}, u32[]{:S(2)}) %copy-start) | copy-done | bytes 2097176
  15.5 1.3 %shard_map.65 = (bf16[256,1024]{1,0:T(8,128)(2,1)S(1)}, bf16[256,1024]{1,0:T(8,128)(2,1)}, bf16[256,1024]{1,0:T(8,128)(2,1)}, bf16[256,1024]{1,0:T(8,128)(2,1)}) custom-call(bf16[1024,1024]{1,0:T(8,128)(2,1)S(1)} %bitcast.17), custom_call_target="tpu_custom_call" | custom-call | tf_op jit(solution)/shard_map/pallas_call | solution.py:165
  16.8 3.1 %collective-permute-start = (bf16[256,1024]{1,0:T(8,128)(2,1)}, bf16[256,1024]{1,0:T(8,128)(2,1)S(1)}, u32[]{:S(2)}, u32[]{:S(2)}) collective-permute-start(bf16[256,1024]{1,0:T(8,128)(2,1)} %get-tuple-element.25), channel_id=1, source_target_pairs={{0,128},{128,0},{256,384},{384,256},{1,129},{129,1},{257,385},{385... | collective-permute-start | bytes 1572872 | tf_op jit(solution)/shard_map/ppermute | solution.py:175
  20.0 4.3 %collective-permute-start.1 = (bf16[256,1024]{1,0:T(8,128)(2,1)}, bf16[256,1024]{1,0:T(8,128)(2,1)S(1)}, u32[]{:S(2)}, u32[]{:S(2)}) collective-permute-start(bf16[256,1024]{1,0:T(8,128)(2,1)} %get-tuple-element.26), channel_id=1, source_target_pairs={{0,256},{128,384},{256,0},{384,128},{1,257},{129,385},{257,1},{385... | collective-permute-start | bytes 1572872 | tf_op jit(solution)/shard_map/ppermute | solution.py:175
  24.3 2.1 %collective-permute-start.2 = (bf16[256,1024]{1,0:T(8,128)(2,1)}, bf16[256,1024]{1,0:T(8,128)(2,1)}, u32[]{:S(2)}, u32[]{:S(2)}) collective-permute-start(bf16[256,1024]{1,0:T(8,128)(2,1)} %get-tuple-element.27), channel_id=1, source_target_pairs={{0,384},{128,256},{256,128},{384,0},{1,385},{129,257},{257,129},{3... | collective-permute-start | bytes 1572872 | tf_op jit(solution)/shard_map/ppermute | solution.py:175
  26.4 0.1 reshape.54
  26.5 0.1 copy.17
  26.6 0.1 reshape.55.columns_ref
  26.7 0.1 mul.114
  26.8 0.1 dynamic_slice.8.order_ref
  26.9 0.6 fusion.9
  27.5 0.7 all-to-all-done
  28.2 0.7 copy.28
  28.9 10.6 %all-to-all-start.1 = ((bf16[16,8,256]{2,1,0:T(8,128)(2,1)}), bf16[16,8,256]{2,1,0:T(8,128)(2,1)S(1)}, u32[]{:S(2)}, u32[]{:S(2)}) async-start(bf16[16,8,256]{2,1,0:T(8,128)(2,1)} %bitcast.16), calls=%async_computation.1 | async-start | bytes 131072 | tf_op jit(solution)/shard_map/all_to_all | solution.py:28
  39.5 0.2 reshape.52
  39.8 0.1 fusion.22
  39.8 0.1 copy.24
  39.9 0.1 copy.23
  40.0 2.2 %sine_multiply_fusion = (f32[64,1024]{1,0:T(8,128)S(1)}, f32[64,1024]{1,0:T(8,128)S(1)}, f32[64,1024]{1,0:T(8,128)S(1)}, f32[64,1024]{1,0:T(8,128)S(1)}) fusion(s32[1024]{0:T(1024)S(1)} %fusion.20, s32[64]{0:T(128)S(1)} %bitcast.24, s32[64]{0:T(128)S(1)} %bitcast.25), kind=kLoop, calls=%fused_computation.16 | loop fusion | flops 2097152 | bytes 1053184 | tf_op jit(solution)/shard_map/mul | solution.py:279
  42.1 1.2 %reshape.51.legendre_ref = bf16[256,1024]{1,0:T(8,128)(2,1)S(1)} reshape(bf16[64,4,1024]{2,1,0:T(4,128)(2,1)} %copy-done.2) | data formatting | bytes 1048576 | tf_op jit(solution)/shard_map/reshape | solution.py:293
  43.3 4.0 %all-to-all-done.1.x_ref = bf16[16,8,256]{2,1,0:T(8,128)(2,1)S(1)} async-done(((bf16[16,8,256]{2,1,0:T(8,128)(2,1)}), bf16[16,8,256]{2,1,0:T(8,128)(2,1)S(1)}, u32[]{:S(2)}, u32[]{:S(2)}) %all-to-all-start.1) | async-done | bytes 65568 | tf_op jit(solution)/shard_map/all_to_all | solution.py:28
  47.3 2.8 %shard_map.64 = f32[64,256]{1,0:T(8,128)S(1)} custom-call(s32[16]{0:T(128)S(1)} %copy-done.1, bf16[16,8,256]{2,1,0:T(8,128)(2,1)S(1)} %all-to-all-done.1.x_ref, f32[26,1024]{1,0:T(8,128)S(1)} %get-tuple-element.36.cos_ref, f32[26,1024]{1,0:T(8,128)S(1)} %get-tuple-element.35.sin_ref, s32[1,1024]{1,0:T(1,128)S(1)} %reshape.55.columns_ref), custom_call_target="tpu_custom_call" | custom-call | tf_op jit(solution)/shard_map/pallas_call | solution.py:136
  50.2 0.1 copy.19
  50.3 14.5 %all_to_all.42 = f32[64,1,256]{2,1,0:T(1,128)S(1)} all-to-all(f32[64,1,256]{2,1,0:T(1,128)S(1)} %copy.19), channel_id=1, replica_groups=mesh['x'=4,'z'=8,'ya'=8,'yb'=2] {'x','ya','yb'}, dimensions={0} | all-to-all | bytes 131072 | tf_op jit(solution)/shard_map/all_to_all | solution.py:28
  64.8 1.6 %shard_map.66 = bf16[8,32,1024]{2,1,0:T(8,128)(2,1)S(1)} custom-call(s32[16]{0:T(128)S(1)} %dynamic_slice.8.order_ref, f32[64,256]{1,0:T(8,128)S(1)} %bitcast.18, bf16[256,1024]{1,0:T(8,128)(2,1)S(1)} %get-tuple-element.24.refs_0_, bf16[256,1024]{1,0:T(8,128)(2,1)S(1)} %collective-permute-done.refs_1_, bf16[256,1024]{1,0:T(8,128)(2,1)S(1)} %collective-permute-done.1.refs_2_, ...), custom_call_target="tpu_custom_call" | custom-call | tf_op jit(solution)/shard_map/pallas_call | solution.py:196
  66.4 21.7 %all_to_all.43.sums_ref = bf16[8,32,1024]{2,1,0:T(8,128)(2,1)S(1)} all-to-all(bf16[8,32,1024]{2,1,0:T(8,128)(2,1)S(1)} %shard_map.66), channel_id=1, replica_groups=mesh['x'=4,'z'=8,'ya'=8,'yb'=2] {'z'}, dimensions={0} | all-to-all | bytes 1048576 | tf_op jit(solution)/shard_map/all_to_all | solution.py:28
  88.2 0.6 shard_map.67
  88.8 14.4 %all_to_all.44 = f32[64,1,128]{2,1,0:T(1,128)S(1)} all-to-all(f32[64,1,128]{2,1,0:T(1,128)S(1)} %bitcast.21), channel_id=1, replica_groups=mesh['x'=4,'z'=8,'ya'=8,'yb'=2] {'yb','x','z'}, dimensions={0} | all-to-all | bytes 65536 | tf_op jit(solution)/shard_map/all_to_all | solution.py:28
  103.1 1.0 shard_map.68
  104.2 10.1 %all_to_all.45 = f32[8,8,4,128]{3,2,1,0:T(4,128)S(1)} all-to-all(f32[8,8,4,128]{3,2,1,0:T(4,128)S(1)} %shard_map.68), channel_id=1, replica_groups=mesh['x'=4,'z'=8,'ya'=8,'yb'=2] {'ya'}, dimensions={0} | all-to-all | bytes 262144 | tf_op jit(solution)/shard_map/all_to_all | solution.py:28
  114.3 0.6 reduce_sum.9
  (17 shorter events, 0.1 us)
Async XLA Ops:
  0.0 26.9 %copy-start.5 = (s32[26]{0:T(128)S(1)}, s32[26]{0:T(128)}, u32[]{:S(2)}) copy-start(s32[26]{0:T(128)} %constant.105.clone) | copy-start | bytes 316
  0.0 26.4 %copy-start.4 = (s32[1024]{0:T(1024)S(1)}, s32[1024]{0:T(1024)}, u32[]{:S(2)}) copy-start(s32[1024]{0:T(1024)} %param.8) | copy-start | bytes 12292
  0.0 28.2 %copy-start.3 = (bf16[8,16,256]{2,1,0:T(8,128)(2,1)S(1)}, bf16[8,16,256]{2,1,0:T(8,128)(2,1)}, u32[]{:S(2)}) copy-start(bf16[8,16,256]{2,1,0:T(8,128)(2,1)} %param.6) | copy-start | bytes 196612
  0.0 28.2 %all-to-all-start = ((bf16[64,4,1024]{2,1,0:T(4,128)(2,1)}), bf16[64,4,1024]{2,1,0:T(4,128)(2,1)S(1)}, u32[]{:S(2)}, u32[]{:S(2)}) async-start(bf16[64,4,1024]{2,1,0:T(4,128)(2,1)} %param.10), calls=%async_computation | async-start | bytes 1048576 | tf_op jit(solution)/shard_map/all_to_all | solution.py:28
  13.9 1.6 %copy-start = (bf16[64,16,1024]{2,1,0:T(8,128)(2,1)S(1)}, bf16[64,16,1024]{2,1,0:T(8,128)(2,1)}, u32[]{:S(2)}) copy-start(bf16[64,16,1024]{2,1,0:T(8,128)(2,1)} %param.9) | copy-start | bytes 6291460
  16.8 30.5 %copy-start.1 = (s32[16]{0:T(128)S(1)}, s32[16]{0:T(128)}, u32[]{:S(2)}) copy-start(s32[16]{0:T(128)} %cycle_ref.1) | copy-start | bytes 196
  16.8 47.9 %collective-permute-start = (bf16[256,1024]{1,0:T(8,128)(2,1)}, bf16[256,1024]{1,0:T(8,128)(2,1)S(1)}, u32[]{:S(2)}, u32[]{:S(2)}) collective-permute-start(bf16[256,1024]{1,0:T(8,128)(2,1)} %get-tuple-element.25), channel_id=1, source_target_pairs={{0,128},{128,0},{256,384},{384,256},{1,129},{129,1},{257,385},{385... | collective-permute-start | bytes 1572872 | tf_op jit(solution)/shard_map/ppermute | solution.py:175
  20.0 44.8 %collective-permute-start.1 = (bf16[256,1024]{1,0:T(8,128)(2,1)}, bf16[256,1024]{1,0:T(8,128)(2,1)S(1)}, u32[]{:S(2)}, u32[]{:S(2)}) collective-permute-start(bf16[256,1024]{1,0:T(8,128)(2,1)} %get-tuple-element.26), channel_id=1, source_target_pairs={{0,256},{128,384},{256,0},{384,128},{1,257},{129,385},{257,1},{385... | collective-permute-start | bytes 1572872 | tf_op jit(solution)/shard_map/ppermute | solution.py:175
  24.3 40.5 %collective-permute-start.2 = (bf16[256,1024]{1,0:T(8,128)(2,1)}, bf16[256,1024]{1,0:T(8,128)(2,1)}, u32[]{:S(2)}, u32[]{:S(2)}) collective-permute-start(bf16[256,1024]{1,0:T(8,128)(2,1)} %get-tuple-element.27), channel_id=1, source_target_pairs={{0,384},{128,256},{256,128},{384,0},{1,385},{129,257},{257,129},{3... | collective-permute-start | bytes 1572872 | tf_op jit(solution)/shard_map/ppermute | solution.py:175
  28.2 11.8 %copy-start.2 = (bf16[64,4,1024]{2,1,0:T(4,128)(2,1)}, bf16[64,4,1024]{2,1,0:T(4,128)(2,1)S(1)}, u32[]{:S(2)}) copy-start(bf16[64,4,1024]{2,1,0:T(4,128)(2,1)S(1)} %all-to-all-done) | copy-start | bytes 1572868
  28.9 18.4 %all-to-all-start.1 = ((bf16[16,8,256]{2,1,0:T(8,128)(2,1)}), bf16[16,8,256]{2,1,0:T(8,128)(2,1)S(1)}, u32[]{:S(2)}, u32[]{:S(2)}) async-start(bf16[16,8,256]{2,1,0:T(8,128)(2,1)} %bitcast.16), calls=%async_computation.1 | async-start | bytes 131072 | tf_op jit(solution)/shard_map/all_to_all | solution.py:28
